TPU v7x, 32 devices: a whole 2x2x4 slice. The times are simulated.
32 devices in a mesh: groups: 2 (over y), xfer: 4 (over x, core), tensor: 4 (over z).
Axes of the slice: x: 2, y: 2, z: 4, core: 2. Of those that a mesh axis runs over, the one named last changes fastest.
Arguments:
- kv_values: bfloat16 [131072, 576], P(('groups', 'xfer', 'tensor')), parts along dimension 0, may hold values from -8 to 8
- kv_scales: bfloat16 [131072, 4], P(('groups', 'xfer', 'tensor')), parts along dimension 0, may hold values from 0.29882812 to 3
- decode_of: int32 [256], P('groups'), parts along dimension 0, may hold values from 0 to 3, as said below
- kv_lengths: int32 [256], P('groups'), parts along dimension 0, may hold values from 1 to 512, as said below
- q_nope: bfloat16 [256, 4, 16384], P(('groups', 'xfer'), None, 'tensor'), parts along dimension 0, may hold values from -6 to 6
- q_rope: bfloat16 [256, 4, 8192], P(('groups', 'xfer'), None, 'tensor'), parts along dimension 0, may hold values from -8 to 8
- new_kv: bfloat16 [256, 4, 576], P(('groups', 'xfer')), parts along dimension 0, may hold values from -6 to 6
- wk_up: bfloat16 [128, 128, 512], P('tensor'), may hold values from -0.5 to 0.5
- wv_up: bfloat16 [128, 512, 128], P('tensor'), may hold values from -0.25 to 0.25
- w_out: bfloat16 [16384, 3584], P('tensor'), may hold values from -0.046875 to 0.046875
Outputs:
- attn_output: bfloat16 [256, 4, 3584], P(('groups', 'xfer', 'tensor')), parts along dimension 0
There are 2 independent parts, one for each index of `groups`. A program takes and returns all parts, laid end to end along the dimension named above; an argument that names none is the same for every part. Nothing has to cross between parts.
Inputs may be any that keep to these rules, and one draw needn't show every extreme that they name: `decode_of`: requests i * 32 to (i + 1) * 32 - 1 were prefilled by group i. Every decode group is named by exactly 32 requests. From each prefill group 8 requests go to each decode group, except for two crossed pairs of prefill and decode groups: two pairs carry 12 requests and the two opposite pairs 8 - 4. `kv_lengths`: some request has length 512.
All inputs are finite; a program needn't handle non-finite values.
Results may differ from a plain program's by a relative error of at most 0.012.
Values may be sent and summed in bfloat16 or wider, within the bound.
No kernel may reach another device: no remote copies, remote signals or barrier semaphores. Data moves between devices by JAX's collectives and lax.ppermute only.
A program may use at most 192 MiB of HBM per device.

v0:
```python
import math

import jax
import jax.numpy as jnp
from jax import lax
from jax.sharding import PartitionSpec as P

MASKED_SCORE = -1e30


def dequantize(values, scales, latent_width):
    latent = values[..., :latent_width].astype(jnp.float32)
    leading = latent.shape[:-1]
    blocks = scales.shape[-1]
    latent = (
        latent.reshape(leading + (blocks, latent_width // blocks))
        * scales.astype(jnp.float32)[..., None]
    )
    latent = latent.reshape(leading + (latent_width,)).astype(jnp.bfloat16)
    return jnp.concatenate([latent, values[..., latent_width:]], axis=-1)


def attend_block(running, queries, key_rows, live_mask, score_scale, latent_width):
    running_max, weight_sum, accumulated = running
    scores = (
        jnp.einsum("rqc,rkc->rqk", queries, key_rows, preferred_element_type=jnp.float32)
        * score_scale
    )
    block_top = jnp.max(jnp.where(live_mask, scores, MASKED_SCORE), axis=-1)
    new_top = jnp.maximum(running_max, block_top)
    exp_weights = jnp.where(live_mask, jnp.exp(scores - new_top[..., None]), 0.0)
    factor = jnp.exp(running_max - new_top)
    weight_sum = jnp.sum(exp_weights, axis=-1)
    accumulated = jnp.einsum(
        "rqk,rkc->rqc",
        exp_weights.astype(jnp.bfloat16),
        key_rows[..., :latent_width],
        preferred_element_type=jnp.float32,
    )
    return (new_top, weight_sum, accumulated)


def empty_carry(rows, query_rows, latent_width):
    return (
        jnp.full((rows, query_rows), MASKED_SCORE, jnp.float32),
        jnp.zeros((rows, query_rows), jnp.float32),
        jnp.zeros((rows, query_rows, latent_width), jnp.float32),
    )


def local(kv_values, kv_scales, decode_of, kv_lengths, q_nope, q_rope, new_kv, wk_up, wv_up, w_out):
    groups = lax.axis_size("xfer")
    shards = lax.axis_size("tensor")
    my_group = lax.axis_index("xfer")
    requests = decode_of.shape[0]
    per_group = requests // groups
    row_width = kv_values.shape[1]
    shard_span = kv_values.shape[0] // per_group
    blocks = kv_scales.shape[1]
    pair_share = per_group // groups
    pair_room = pair_share + pair_share // 2
    heads_here = wk_up.shape[0]
    latent_width = wk_up.shape[2]
    step_count = q_nope.shape[1]
    score_scale = 1.0 / math.sqrt(q_nope.shape[2] // heads_here + q_rope.shape[2] // heads_here)
    out_rows = per_group // shards
    targets = jnp.arange(groups, dtype=jnp.int32)
    dest_hot = (decode_of[:, None] == targets[None, :]).astype(jnp.int32)
    slot_all = jnp.sum((jnp.cumsum(dest_hot, axis=0) - dest_hot) * dest_hot, axis=1)
    pair_hot = dest_hot.reshape(groups, per_group, groups)
    pair_rank = jnp.sum((jnp.cumsum(pair_hot, axis=1) - pair_hot) * pair_hot, axis=2).reshape(
        requests
    )
    request_ids = jnp.arange(requests, dtype=jnp.int32)
    owner_group = request_ids // per_group
    mine_dest = lax.dynamic_slice_in_dim(decode_of, my_group * per_group, per_group)
    mine_rank = lax.dynamic_slice_in_dim(pair_rank, my_group * per_group, per_group)
    outgoing = jnp.arange(groups * pair_room, dtype=jnp.int32)
    send_match = (outgoing[:, None] == (mine_dest * pair_room + mine_rank)[None, :]).astype(
        jnp.int32
    )
    send_index = jnp.sum(send_match * jnp.arange(per_group, dtype=jnp.int32)[None, :], axis=1)
    slot_ids = jnp.arange(per_group, dtype=jnp.int32)
    take_match = (
        (decode_of[None, :] == my_group) & (slot_all[None, :] == slot_ids[:, None])
    ).astype(jnp.int32)
    served = jnp.sum(take_match * request_ids[None, :], axis=1)
    recv_index = jnp.take(owner_group, served) * pair_room + jnp.take(pair_rank, served)
    lengths = jnp.take(kv_lengths, served)
    regions = kv_values.reshape(per_group, shard_span, row_width)
    region_scales = kv_scales.reshape(per_group, shard_span, blocks)
    packed = jnp.take(regions, send_index, axis=0).reshape(groups, pair_room, shard_span, row_width)
    packed_scales = jnp.take(region_scales, send_index, axis=0).reshape(
        groups, pair_room, shard_span, blocks
    )
    arrived, arrived_scales = (
        lax.all_to_all(packed, "xfer", split_axis=0, concat_axis=0, tiled=True),
        lax.all_to_all(packed_scales, "xfer", split_axis=0, concat_axis=0, tiled=True),
    )
    local_values = jnp.take(
        arrived.reshape(groups * pair_room, shard_span, row_width), recv_index, axis=0
    )
    local_scales = jnp.take(
        arrived_scales.reshape(groups * pair_room, shard_span, blocks), recv_index, axis=0
    )
    local_cache = dequantize(local_values, local_scales, latent_width)
    query_heads = q_nope.reshape(per_group, step_count, heads_here, -1)
    query_latent = jnp.einsum(
        "rthn,hnc->rthc", query_heads, wk_up, preferred_element_type=jnp.float32
    ).astype(jnp.bfloat16)
    queries = jnp.concatenate(
        [query_latent, q_rope.reshape(per_group, step_count, heads_here, -1)], axis=-1
    )
    slot_keys = lax.all_to_all(local_cache, "tensor", split_axis=0, concat_axis=1, tiled=True)
    slot_queries = lax.all_to_all(queries, "tensor", split_axis=0, concat_axis=2, tiled=True)
    all_heads = slot_queries.shape[2]
    query_rows = step_count * all_heads
    flat_queries = slot_queries.reshape(out_rows, query_rows, row_width)
    first_slot = lax.axis_index("tensor") * out_rows
    slot_new = lax.dynamic_slice_in_dim(new_kv, first_slot, out_rows, 0)
    slot_lengths = lax.dynamic_slice_in_dim(lengths, first_slot, out_rows, 0)
    key_rows = jnp.concatenate([slot_keys, slot_new], axis=1)
    cache_rows = slot_keys.shape[1]
    position = jnp.arange(cache_rows, dtype=jnp.int32)
    live_cache = jnp.broadcast_to(
        (position[None, :] < slot_lengths[:, None])[:, None, :], (out_rows, query_rows, cache_rows)
    )
    query_step = jnp.arange(query_rows, dtype=jnp.int32) // all_heads
    causal = query_step[:, None] >= jnp.arange(step_count, dtype=jnp.int32)[None, :]
    live_new = jnp.broadcast_to(causal[None, :, :], (out_rows, query_rows, step_count))
    live_mask = jnp.concatenate([live_cache, live_new], axis=2)
    running_max, weight_sum, accumulated = attend_block(
        empty_carry(out_rows, query_rows, latent_width),
        flat_queries,
        key_rows,
        live_mask,
        score_scale,
        latent_width,
    )
    slot_latent = (
        (accumulated / weight_sum[..., None])
        .astype(jnp.bfloat16)
        .reshape(out_rows, step_count, all_heads, latent_width)
    )
    mixed = lax.all_to_all(slot_latent, "tensor", split_axis=2, concat_axis=0, tiled=True)
    head_out = jnp.einsum(
        "rthc,hcv->rthv", mixed, wv_up, preferred_element_type=jnp.float32
    ).astype(jnp.bfloat16)
    head_out = head_out.reshape(per_group, step_count, -1)
    partial_sum = jnp.dot(head_out, w_out, preferred_element_type=jnp.float32)
    summed = lax.psum(partial_sum.astype(jnp.bfloat16), "tensor").astype(jnp.float32)
    return lax.dynamic_slice_in_dim(
        summed, lax.axis_index("tensor") * out_rows, out_rows, 0
    ).astype(jnp.bfloat16)


def solution(mesh):
    return jax.shard_map(
        local,
        mesh=mesh,
        in_specs=(
            P(("groups", "xfer", "tensor"), None),
            P(("groups", "xfer", "tensor"), None),
            P("groups"),
            P("groups"),
            P(("groups", "xfer"), None, "tensor"),
            P(("groups", "xfer"), None, "tensor"),
            P(("groups", "xfer"), None, None),
            P("tensor", None, None),
            P("tensor", None, None),
            P("tensor", None),
        ),
        out_specs=P(("groups", "xfer", "tensor"), None, None),
        check_vma=False,
    )
```

profile of v0, /device:TPU:0, one launch (start us, length us, event | category | flops | bytes accessed | tf_op | source)
XLA Modules:
  0.0 540.6 jit_solution(13673256578127582203)
XLA Ops:
  8.7 1.4 gather_fusion.2
  10.9 4.2 all-to-all-start.2
  15.1 5.9 %copy_bitcast_fusion = bf16[32,128,576]{1,2,0:T(8,128)(2,1)} fusion(bf16[4096,576]{0,1:T(8,128)(2,1)} %param.12), kind=kLoop, calls=%fused_computation.24 | loop fusion | bytes 9437184 | tf_op jit(solution)/shard_map/reshape | solution.py:90
  20.9 7.7 %gather_fusion = bf16[48,128,576]{1,2,0:T(8,128)(2,1)} fusion(bf16[32,128,576]{1,2,0:T(8,128)(2,1)} %copy_bitcast_fusion, s32[1024]{0:T(1024)S(1)} %pad_clamp_fusion.1), kind=kCustom, calls=%fused_computation.3 | custom fusion | bytes 14155968 | tf_op jit(solution)/shard_map/jit(_take)/gather | solution.py:92
  28.6 6.7 %broadcast_select_fusion = bf16[4,12,128,576]{2,3,1,0:T(8,128)(2,1)} fusion(bf16[4,12,128,576]{2,3,1,0:T(8,128)(2,1)} %bitcast.69, pred[4,12]{1,0:T(4,128)(4,1)S(1)} %compare_and_fusion.1), kind=kLoop, calls=%fused_computation.15 | loop fusion | flops 3538944 | bytes 14155824 | tf_op jit(solution)/shard_map/jit(_take)/select_n | solution.py:92
  35.3 5.5 %all-to-all-start.1 = ((bf16[4,12,128,576]{2,3,1,0:T(8,128)(2,1)}), bf16[4,12,128,576]{2,3,1,0:T(8,128)(2,1)}, u32[]{:S(2)}, u32[]{:S(2)}) async-start(bf16[4,12,128,576]{2,3,1,0:T(8,128)(2,1)} %broadcast_select_fusion), calls=%async_computation.1 | async-start | bytes 14155776 | tf_op jit(solution)/shard_map/all_to_all | solution.py:97
  40.9 1.1 reshape.139
  42.0 0.8 reshape.219
  43.5 3.8 convert_bitcast_fusion
  47.3 0.8 pad_maximum_fusion
  48.1 5.0 copy.49
  53.1 66.9 %all-to-all-done.1 = bf16[4,12,128,576]{2,3,1,0:T(8,128)(2,1)} async-done(((bf16[4,12,128,576]{2,3,1,0:T(8,128)(2,1)}), bf16[4,12,128,576]{2,3,1,0:T(8,128)(2,1)}, u32[]{:S(2)}, u32[]{:S(2)}) %all-to-all-start.1) | async-done | bytes 7077920 | tf_op jit(solution)/shard_map/all_to_all | solution.py:97
  120.0 5.4 all-to-all-start
  128.2 6.3 %gather_fusion.1 = bf16[32,128,576]{1,2,0:T(8,128)(2,1)} fusion(bf16[48,128,576]{1,2,0:T(8,128)(2,1)} %bitcast.9, s32[1024]{0:T(1024)S(1)} %pad_clamp_fusion), kind=kCustom, calls=%fused_computation.4 | custom fusion | bytes 9437312 | tf_op jit(solution)/shard_map/jit(_take)/gather | solution.py:100
  134.5 2.9 broadcast_select_fusion.1
  137.4 1.2 fusion.2
  138.6 2.5 pad_maximum_fusion.1
  141.2 100.3 %all-to-all-done = bf16[32,4,32,576]{3,1,2,0:T(4,128)(2,1)} async-done(((bf16[32,4,32,576]{3,1,2,0:T(4,128)(2,1)}), bf16[32,4,32,576]{3,1,2,0:T(4,128)(2,1)}, u32[]{:S(2)}, u32[]{:S(2)}) %all-to-all-start) | async-done | bytes 4718624 | tf_op jit(solution)/shard_map/all_to_all | solution.py:115
  241.5 5.0 all-to-all-start.3
  247.5 5.9 %copy.50 = bf16[4,8,4,32,576]{4,3,0,2,1:T(8,128)(2,1)} copy(bf16[4,8,4,32,576]{4,2,3,1,0:T(4,128)(2,1)} %bitcast.3) | data formatting | bytes 9437184 | tf_op jit(solution)/shard_map/all_to_all | solution.py:115
  253.4 97.1 %all-to-all-done.3 = bf16[32,128,576]{1,2,0:T(8,128)(2,1)} async-done(((bf16[32,128,576]{1,2,0:T(8,128)(2,1)}), bf16[32,128,576]{1,2,0:T(8,128)(2,1)}, u32[]{:S(2)}, u32[]{:S(2)}) %all-to-all-start.3) | async-done | bytes 4718624 | tf_op jit(solution)/shard_map/all_to_all | solution.py:114
  350.5 7.7 %copy.52 = bf16[8,4,128,576]{3,2,1,0:T(8,128)(2,1)} copy(bf16[8,4,128,576]{2,3,0,1:T(8,128)(2,1)} %bitcast.15) | data formatting | bytes 9437184 | tf_op jit(solution)/shard_map/all_to_all | solution.py:114
  358.9 6.6 %select_reduce_fusion = (f32[8,512]{1,0:T(8,128)S(1)}, f32[8,512,516]{1,2,0:T(8,128)S(1)}) fusion(pred[8,512,4]{1,2,0:T(4,128)(4,1)S(1)} %broadcast_in_dim.87, pred[8,512,512]{1,2,0:T(8,128)(4,1)S(1)} %broadcast_in_dim.86, bf16[8,512,576]{2,1,0:T(8,128)(2,1)} %bitcast.71, bf16[8,4,576]{2,1,0:T(4,128)(2,1)S(1)} %constant_dynamic-slice_fusion, ...), kind=kOutput, calls=%fused_computation.10 | convolution fusion | flops 2452754432 | bytes 20058112 | tf_op jit(solution)/shard_map/rqc,rkc->rqk/dot_general | solution.py:26
  365.6 2.3 fusion.7
  368.1 5.1 divide_convert_fusion
  373.2 3.2 copy.54
  376.4 95.6 %all_to_all.61 = bf16[8,4,128,512]{3,1,0,2:T(4,128)(2,1)S(1)} all-to-all(bf16[8,4,128,512]{3,1,0,2:T(4,128)(2,1)S(1)} %copy.54), channel_id=1, replica_groups=mesh['groups'=2,'xfer'=4,'tensor'=4] {'tensor'}, dimensions={2} | all-to-all | bytes 8388608 | tf_op jit(solution)/shard_map/all_to_all | solution.py:145
  472.1 1.3 fusion.37
  473.4 12.5 %fusion.9 = bf16[32,4,3584]{2,0,1:T(8,128)(2,1)} fusion(bf16[4096,3584]{1,0:T(8,128)(2,1)} %param.21, bf16[32,4,4,8,128]{4,3,2,1,0:T(8,128)(2,1)S(1)} %fusion.37), kind=kOutput, calls=%fused_computation.23 | convolution fusion | flops 3758555136 | bytes 31326208 | tf_op jit(solution)/shard_map/dot_general | solution.py:150
  485.9 46.1 %all-reduce.2.cloned.1.call-done = bf16[32,4,3584]{2,0,1:T(8,128)(2,1)} async-done(((bf16[32,4,3584]{2,0,1:T(8,128)(2,1)}), bf16[32,4,3584]{2,0,1:T(8,128)(2,1)}) %all-reduce.2.cloned.1.call-update) | async-done | bytes 917520 | tf_op jit(solution)/shard_map/psum | solution.py:151
  532.0 1.0 convert_convert_fusion
  533.0 0.8 copy.57
  (57 shorter events, 8.2 us)
Async XLA Ops:
  6.5 240.8 %copy-start = (bf16[32,4,576]{2,1,0:T(4,128)(2,1)S(1)}, bf16[32,4,576]{2,1,0:T(4,128)(2,1)}, u32[]{:S(2)}) copy-start(bf16[32,4,576]{2,1,0:T(4,128)(2,1)} %param.18) | copy-start | bytes 442372
  10.9 24.5 %all-to-all-start.2 = ((bf16[4,12,128,4]{2,3,1,0:T(4,128)(2,1)}), bf16[4,12,128,4]{2,3,1,0:T(4,128)(2,1)S(1)}, u32[]{:S(2)}, u32[]{:S(2)}) async-start(bf16[4,12,128,4]{2,3,1,0:T(4,128)(2,1)} %broadcast_select_fusion.2), calls=%async_computation.2 | async-start | bytes 98304 | tf_op jit(solution)/shard_map/all_to_all | solution.py:98
  35.3 5.5 %copy-start.4 = (bf16[32,4,4096]{2,1,0:T(4,128)(2,1)S(1)}, bf16[32,4,4096]{2,1,0:T(4,128)(2,1)}, u32[]{:S(2)}) copy-start(bf16[32,4,4096]{2,1,0:T(4,128)(2,1)} %param.16) | copy-start | bytes 3145732
  35.3 6.7 %copy-start.5 = (bf16[32,4,2048]{2,1,0:T(4,128)(2,1)S(1)}, bf16[32,4,2048]{2,1,0:T(4,128)(2,1)}, u32[]{:S(2)}) copy-start(bf16[32,4,2048]{2,1,0:T(4,128)(2,1)} %param.17) | copy-start | bytes 1572868
  35.3 84.7 %all-to-all-start.1 = ((bf16[4,12,128,576]{2,3,1,0:T(8,128)(2,1)}), bf16[4,12,128,576]{2,3,1,0:T(8,128)(2,1)}, u32[]{:S(2)}, u32[]{:S(2)}) async-start(bf16[4,12,128,576]{2,3,1,0:T(8,128)(2,1)} %broadcast_select_fusion), calls=%async_computation.1 | async-start | bytes 14155776 | tf_op jit(solution)/shard_map/all_to_all | solution.py:97
  53.1 72.3 %copy-start.6 = (s32[128]{0:T(128)S(1)}, s32[128]{0:T(128)}, u32[]{:S(2)}) copy-start(s32[128]{0:T(128)} %param.14) | copy-start | bytes 1540
  120.0 121.5 %all-to-all-start = ((bf16[32,4,32,576]{3,1,2,0:T(4,128)(2,1)}), bf16[32,4,32,576]{3,1,2,0:T(4,128)(2,1)}, u32[]{:S(2)}, u32[]{:S(2)}) async-start(bf16[32,4,32,576]{3,1,2,0:T(4,128)(2,1)} %copy.49), calls=%async_computation | async-start | bytes 10485760 | tf_op jit(solution)/shard_map/all_to_all | solution.py:115
  141.2 105.4 %copy-start.2 = (s32[128]{0:T(128)S(1)}, s32[128]{0:T(128)}, u32[]{:S(2)}) copy-start(s32[128]{0:T(128)} %param.15) | copy-start | bytes 1540
  241.5 109.0 %all-to-all-start.3 = ((bf16[32,128,576]{1,2,0:T(8,128)(2,1)}), bf16[32,128,576]{1,2,0:T(8,128)(2,1)}, u32[]{:S(2)}, u32[]{:S(2)}) async-start(bf16[32,128,576]{1,2,0:T(8,128)(2,1)} %pad_maximum_fusion.1), calls=%async_computation.3 | async-start | bytes 9437184 | tf_op jit(solution)/shard_map/all_to_all | solution.py:114
  246.5 285.5 %all-reduce.2.cloned.1.call-start = ((), (), s32[]{:S(2)}) async-start(), calls=%async_computation.5 | async-start | bytes 1835008 | tf_op jit(solution)/shard_map/psum | solution.py:151
  365.6 2.5 copy-start.3
  376.4 95.6 %copy-start.7 = (bf16[32,512,128]{2,1,0:T(8,128)(2,1)S(1)}, bf16[32,512,128]{2,1,0:T(8,128)(2,1)}, u32[]{:S(2)}) copy-start(bf16[32,512,128]{2,1,0:T(8,128)(2,1)} %param.20) | copy-start | bytes 12582916
  473.4 60.4 %copy-start.1 = (bf16[32,4,576]{2,1,0:T(4,128)(2,1)S(1)}, bf16[32,4,576]{2,1,0:T(4,128)(2,1)}, u32[]{:S(2)}) copy-start(bf16[32,4,576]{2,1,0:T(4,128)(2,1)} %param.18) | copy-start | bytes 442372
Sparse Core Ops, SparseCore 0:
  486.0 45.9 all-reduce.1
where the time goes:
time: 542 us; the launch traced here: 541 us
  waiting for transfers between devices  310 us (57%)
  blocking collectives  95.6 us (18%)
  local copies, waits for them, and re-layouts  51.3 us (9%)
  matrix products  29.3 us (5%)
  starting transfers between devices  20.2 us (4%)
  other arithmetic  20.1 us (4%)
  between operations  13.7 us (3%)
    all_to_all x1, waiting for transfers between devices, local(): lax.all_to_all(queries, 'tensor', split_axis=0, concat_axis=2, tiled=True)  100 us
    all_to_all x1, waiting for transfers between devices, local(): lax.all_to_all(local_cache, 'tensor', split_axis=0, concat_axis=1, tiled=...  97.1 us
    all_to_all x1, blocking collectives, local(): lax.all_to_all(slot_latent, 'tensor', split_axis=2, concat_axis=0, tiled=...  95.6 us
    all_to_all x1, waiting for transfers between devices, local(): lax.all_to_all(packed, 'xfer', split_axis=0, concat_axis=0, tiled=True)  66.9 us
    psum x1, waiting for transfers between devices, local(): lax.psum(partial_sum.astype(jnp.bfloat16), 'tensor').astype(jnp.float32)  46.1 us
    dot_general x1, matrix products, local(): partial_sum = jnp.dot(head_out, w_out, preferred_element_type=jnp.float32)  12.5 us
  transfers between devices with their start and end apart: 5, of which 4 were waited for; matrix products, arithmetic and copies ran while one was open for 10% of the time, Pallas kernels for 0%

commit v1 on v0

v1 whole, which is shorter than its diff:
```python
import math

import jax
import jax.numpy as jnp
from jax import lax
from jax.experimental import pallas as pl
from jax.experimental.pallas import tpu as pltpu
from jax.sharding import PartitionSpec as P

MASKED_SCORE = -1e30
NEW_ROWS = 16


SHORT = pl.CostEstimate(flops=1024, bytes_accessed=1024, transcendentals=0)


def pack_kernel(groups, blocks, index_ref, *refs):
    values, scales = refs[:groups], refs[groups : 2 * groups]
    outs = refs[len(refs) - groups :]
    for value_ref, scale_ref, out_ref in zip(values, scales, outs):
        width = value_ref.shape[-2]
        latent_width = blocks * 128
        span = value_ref.shape[-1]
        factor = scale_ref[...].reshape(blocks, span).astype(jnp.float32)
        for block in range(blocks):
            rows = slice(block * 128, (block + 1) * 128)
            part = value_ref[..., rows, :].reshape(128, span).astype(jnp.float32)
            out_ref[0, rows, :] = (part * factor[block : block + 1, :]).astype(jnp.bfloat16)
        rest = value_ref[..., latent_width:width, :]
        out_ref[0, latent_width:width, :] = rest.reshape(width - latent_width, span)


def pack(values, scales, index, span, waits=()):
    groups, count = index.shape
    width, blocks = values.shape[-2], scales.shape[-2]

    def spec(rows, group):
        if values.ndim == 2:
            return pl.BlockSpec((rows, span), lambda n, index_ref: (0, index_ref[group, n]))
        return pl.BlockSpec((1, rows, span), lambda n, index_ref: (index_ref[group, n], 0, 0))

    return pl.pallas_call(
        lambda *refs: pack_kernel(groups, blocks, *refs),
        grid_spec=pltpu.PrefetchScalarGridSpec(
            num_scalar_prefetch=1,
            grid=(count,),
            in_specs=[spec(width, g) for g in range(groups)]
            + [spec(blocks, g) for g in range(groups)]
            + [pl.BlockSpec(memory_space=pl.ANY)] * len(waits),
            out_specs=[pl.BlockSpec((1, width, span), lambda n, index_ref: (n, 0, 0))] * groups,
        ),
        out_shape=[jax.ShapeDtypeStruct((count, width, span), jnp.bfloat16)] * groups,
        cost_estimate=SHORT,
    )(index, *([values] * groups), *([scales] * groups), *waits)


def pack_all(values, scales, index, span, *waits):
    groups, count = index.shape
    width, blocks = values.shape[-2], scales.shape[-2]

    def kernel(index_ref, *refs):
        outs = [refs[-1].at[g] for g in range(groups)]
        pack_kernel(groups, blocks, index_ref, *refs[: 2 * groups], *outs)

    def spec(rows, group):
        if values.ndim == 2:
            return pl.BlockSpec((rows, span), lambda n, index_ref: (0, index_ref[group, n]))
        return pl.BlockSpec((1, rows, span), lambda n, index_ref: (index_ref[group, n], 0, 0))

    return pl.pallas_call(
        kernel,
        grid_spec=pltpu.PrefetchScalarGridSpec(
            num_scalar_prefetch=1,
            grid=(count,),
            in_specs=[spec(width, g) for g in range(groups)]
            + [spec(blocks, g) for g in range(groups)]
            + [pl.BlockSpec(memory_space=pl.ANY)] * len(waits),
            out_specs=pl.BlockSpec(
                (groups, 1, width, span), lambda n, index_ref: (0, n, 0, 0)
            ),
        ),
        out_shape=jax.ShapeDtypeStruct((groups, count, width, span), jnp.bfloat16),
        cost_estimate=SHORT,
    )(index, *([values] * groups), *([scales] * groups), *waits)


def held(x, *waits):
    def kernel(*refs):
        pass

    anywhere = pl.BlockSpec(memory_space=pl.ANY)
    return pl.pallas_call(
        kernel,
        in_specs=[anywhere] * (1 + len(waits)),
        out_specs=anywhere,
        out_shape=jax.ShapeDtypeStruct(x.shape, x.dtype),
        input_output_aliases={0: 0},
    )(x, *waits)


def regroup_kernel(count, *refs):
    refs = refs[: 2 * count] + refs[-2:]
    for k in range(count):
        refs[2 * count][k, 0] = refs[k][0]
        refs[2 * count + 1][k, 0] = refs[count + k][0]


def regroup(landed, *waits):
    count, (rows, width, span) = len(landed), landed[0].shape
    half = rows // 2
    own = pl.BlockSpec((1, width, span), lambda n: (n, 0, 0))
    far = pl.BlockSpec((1, width, span), lambda n: (half + n, 0, 0))
    outs = pl.pallas_call(
        lambda *refs: regroup_kernel(count, *refs),
        grid=(half,),
        in_specs=[own] * count
        + [far] * count
        + [pl.BlockSpec(memory_space=pl.ANY)] * len(waits),
        out_specs=[pl.BlockSpec((count, 1, width, span), lambda n: (0, n, 0, 0))] * 2,
        out_shape=[jax.ShapeDtypeStruct((count, half, width, span), jnp.bfloat16)] * 2,
        cost_estimate=SHORT,
    )(*landed, *landed, *waits)
    return tuple(x.reshape(count * half, width, span) for x in outs)


def select_kernel(which_ref, index_ref, *refs):
    n = pl.program_id(0)
    sources = (len(refs) - 2) // 2
    for side in range(2):
        for source in range(sources):

            @pl.when(which_ref[side, n] == source)
            def _(side=side, source=source):
                refs[2 * sources + side][...] = refs[side * sources + source][...]


def select_blocks(arrived, which, index):
    count = index.shape[1]
    width, span = arrived[0].shape[1:]

    def pick(side, source):
        def place(n, which_ref, index_ref):
            return jnp.where(which_ref[side, n] == source, index_ref[side, n], 0), 0, 0

        return pl.BlockSpec((1, width, span), place)

    return pl.pallas_call(
        select_kernel,
        grid_spec=pltpu.PrefetchScalarGridSpec(
            num_scalar_prefetch=2,
            grid=(count,),
            in_specs=[pick(i, j) for i in range(2) for j in range(len(arrived))],
            out_specs=[pl.BlockSpec((1, width, span), lambda n, *refs: (n, 0, 0))] * 2,
        ),
        out_shape=[jax.ShapeDtypeStruct((count, width, span), jnp.bfloat16)] * 2,
        cost_estimate=SHORT,
    )(which, index, *arrived, *arrived)


def in_order(pieces, replica):
    count, shape = len(pieces), pieces[0].shape

    def kernel(replica_ref, *refs):
        out_ref, done = refs[count], refs[count + 1]
        copies = [
            pltpu.make_async_copy(refs[t], out_ref.at[replica_ref[0] ^ t], done.at[t])
            for t in range(count)
        ]
        for copy in copies:
            copy.start()
        for copy in copies:
            copy.wait()

    anywhere = pl.BlockSpec(memory_space=pl.ANY)
    return pl.pallas_call(
        kernel,
        in_specs=[pl.BlockSpec(memory_space=pltpu.SMEM)] + [anywhere] * count,
        out_specs=pl.BlockSpec(memory_space=pltpu.VMEM),
        out_shape=jax.ShapeDtypeStruct((count,) + shape, pieces[0].dtype),
        scratch_shapes=[pltpu.SemaphoreType.DMA((count,))],
        cost_estimate=SHORT,
    )(replica[None], *pieces)


def cut(flat, pieces, which, *waits):
    rows, columns = flat.shape[0] // pieces, flat.shape[1]

    def kernel(which_ref, flat_ref, *refs):
        refs[-1][...] = flat_ref[...]

    return pl.pallas_call(
        kernel,
        grid_spec=pltpu.PrefetchScalarGridSpec(
            num_scalar_prefetch=1,
            grid=(1,),
            in_specs=[pl.BlockSpec((rows, columns), lambda n, which_ref: (which_ref[0], 0))]
            + [pl.BlockSpec(memory_space=pl.ANY)] * len(waits),
            out_specs=pl.BlockSpec((rows, columns), lambda n, which_ref: (0, 0)),
        ),
        out_shape=jax.ShapeDtypeStruct((rows, columns), flat.dtype),
        cost_estimate=SHORT,
    )(which[None], flat, *waits)


def by_side(arrays, index, *waits):
    count = index.shape[1]

    def pick(side, x):
        return pl.BlockSpec(
            (1,) + x.shape[1:], lambda n, index_ref: (index_ref[side, n], 0, 0)
        )

    def kernel(index_ref, *refs):
        for i in range(2 * len(arrays)):
            refs[i - 2 * len(arrays)][...] = refs[i][...]

    return pl.pallas_call(
        kernel,
        grid_spec=pltpu.PrefetchScalarGridSpec(
            num_scalar_prefetch=1,
            grid=(count,),
            in_specs=[pick(side, x) for x in arrays for side in range(2)]
            + [pl.BlockSpec(memory_space=pl.ANY)] * len(waits),
            out_specs=[
                pl.BlockSpec((1,) + x.shape[1:], lambda n, index_ref: (n, 0, 0))
                for x in arrays
                for side in range(2)
            ],
        ),
        out_shape=[
            jax.ShapeDtypeStruct((count,) + x.shape[1:], x.dtype)
            for x in arrays
            for side in range(2)
        ],
        cost_estimate=SHORT,
    )(index, *[x for x in arrays for side in range(2)], *waits)


def attend_kernel(shards, steps, score_scale, scalars, *refs):
    queries = refs[:4]
    keys = refs[4 : 4 + shards]
    new_ref, own_out, other_out = refs[4 + shards], refs[-2], refs[-1]
    own_latent, other_latent, own_rope, other_rope = queries
    latent_width = own_latent.shape[2]
    span = keys[0].shape[2]
    length = scalars[1 + pl.program_id(0)]
    shard = scalars[0]
    key_columns = jnp.concatenate([ref[0] for ref in keys], axis=1)
    new_rows = new_ref[0]
    query = jnp.concatenate([own_latent[0], other_latent[0]], axis=0)
    rope = jnp.concatenate([own_rope[0], other_rope[0]], axis=0)
    across = (((1,), (1,)), ((), ()))
    along = (((1,), (0,)), ((), ()))

    def product(left, right, contract):
        return lax.dot_general(left, right, contract, preferred_element_type=jnp.float32)

    cache_scores = score_scale * (
        product(query, key_columns[:latent_width], along)
        + product(rope, key_columns[latent_width:], along)
    )
    new_scores = score_scale * (
        product(query, new_rows[:, :latent_width], across)
        + product(rope, new_rows[:, latent_width:], across)
    )
    column = lax.broadcasted_iota(jnp.int32, cache_scores.shape, 1)
    position = (shard ^ (column // span)) * span + column % span
    cache_live = position < length
    half = own_latent.shape[1]
    row = lax.broadcasted_iota(jnp.int32, new_scores.shape, 0)
    step = (row % half) // (half // steps)
    new_live = lax.broadcasted_iota(jnp.int32, new_scores.shape, 1) <= step
    cache_scores = jnp.where(cache_live, cache_scores, MASKED_SCORE)
    new_scores = jnp.where(new_live, new_scores, MASKED_SCORE)
    top = jnp.maximum(
        jnp.max(cache_scores, axis=1, keepdims=True), jnp.max(new_scores, axis=1, keepdims=True)
    )
    cache_weights = jnp.where(cache_live, jnp.exp(cache_scores - top), 0.0)
    new_weights = jnp.where(new_live, jnp.exp(new_scores - top), 0.0)
    weight_sum = jnp.sum(cache_weights, axis=1, keepdims=True) + jnp.sum(
        new_weights, axis=1, keepdims=True
    )
    mixed = product(
        cache_weights.astype(jnp.bfloat16), key_columns[:latent_width], across
    ) + product(new_weights.astype(jnp.bfloat16), new_rows[:, :latent_width], along)
    latent = (mixed / weight_sum).astype(jnp.bfloat16)
    own_out[0] = latent[:half]
    other_out[0] = latent[half:]


def attend(scalars, start, queries, keys, new_rows, steps, score_scale, waits):
    count, (half, latent_width) = keys[0].shape[0], queries[0].shape[1:]
    rope_width = queries[2].shape[2]
    width, span = keys[0].shape[1:]
    shards = len(keys)

    def block(rows, columns, first=0):
        return pl.BlockSpec((1, rows, columns), lambda n, scalars: (first + n, 0, 0))

    return pl.pallas_call(
        lambda *refs: attend_kernel(shards, steps, score_scale, *refs),
        grid_spec=pltpu.PrefetchScalarGridSpec(
            num_scalar_prefetch=1,
            grid=(count,),
            in_specs=[block(half, latent_width, start)] * 2
            + [block(half, rope_width, start)] * 2
            + [block(width, span)] * shards
            + [block(NEW_ROWS, width, start)]
            + [pl.BlockSpec(memory_space=pl.ANY)] * len(waits),
            out_specs=[block(half, latent_width)] * 2,
        ),
        out_shape=[jax.ShapeDtypeStruct((count, half, latent_width), jnp.bfloat16)] * 2,
        compiler_params=pltpu.CompilerParams(vmem_limit_bytes=32 * 1024 * 1024),
        cost_estimate=SHORT,
    )(scalars, *queries, *keys, new_rows, *waits)


def local(kv_values, kv_scales, decode_of, kv_lengths, q_nope, q_rope, new_kv, wk_up, wv_up, w_out):
    groups = lax.axis_size("xfer")
    shards = lax.axis_size("tensor")
    me = lax.axis_index("xfer")
    shard = lax.axis_index("tensor")
    parity = shard % 2
    requests = decode_of.shape[0]
    per_group = requests // groups
    row_width = kv_values.shape[1]
    span = kv_values.shape[0] // per_group
    pair_share = per_group // groups
    pair_room = pair_share + pair_share // 2
    sure = pair_share - pair_share // 2
    late = pair_share // 2
    heads_here, nope_width, latent_width = wk_up.shape
    value_width = wv_up.shape[2]
    steps = q_nope.shape[1]
    rope_width = q_rope.shape[2] // heads_here
    score_scale = 1.0 / math.sqrt(nope_width + rope_width)
    out_rows = per_group // shards
    half = per_group // 2
    half_sure = sure // 2
    late_half = (per_group - groups * sure) // 4
    sizes = [2 * half_sure, (groups - 2) * half_sure, late_half, late_half]
    starts = [0, sizes[0], sizes[0] + sizes[1], sizes[0] + sizes[1] + sizes[2]]
    late_start = starts[2]

    def across(x, axis, offset, name="other"):
        with jax.named_scope(f"{name}_{axis if isinstance(axis, str) else 'both'}{offset}"):
            return lax.ppermute(x, axis, [(i, i ^ offset) for i in range(lax.axis_size(axis))])

    dest_here = lax.dynamic_slice_in_dim(decode_of, me * per_group, per_group)
    here = jnp.arange(per_group, dtype=jnp.int32)
    rank_here = jnp.sum(
        ((dest_here[:, None] == dest_here[None, :]) & (here[None, :] < here[:, None])).astype(
            jnp.int32
        ),
        axis=1,
    )
    place_here = dest_here * pair_room + rank_here
    early_ranks = jnp.arange(sure, dtype=jnp.int32)
    early_ranks = (early_ranks + parity * half_sure) % sure
    offsets = jnp.arange(groups, dtype=jnp.int32)
    early_places = (me ^ offsets)[:, None] * pair_room + early_ranks[None, :]
    late_ranks = jnp.arange(late, dtype=jnp.int32)
    middle_places = offsets[:, None] * pair_room + sure + late_ranks[None, :]
    last_places = middle_places + late

    def request_at(places):
        hit = places[..., None] == place_here
        return jnp.sum(jnp.where(hit, here, 0), axis=-1)

    if span % 128 == 0:
        values, scales = kv_values.T, kv_scales.T
    else:
        values = kv_values.reshape(per_group, span, -1).swapaxes(1, 2)
        scales = kv_scales.reshape(per_group, span, -1).swapaxes(1, 2)
    early = pack(values, scales, request_at(early_places), span)
    first = regroup([early[0], across(early[1], "xfer", 1, "early")])
    middle_out = pack_all(values, scales, request_at(middle_places), span, first[0])
    second = regroup(
        [across(held(early[k], first[0]), "xfer", k, "early") for k in range(2, groups)]
    )

    ids = jnp.arange(requests, dtype=jnp.int32)
    source = ids // per_group
    mine = decode_of == me
    before = ids[None, :] < ids[:, None]
    rank = jnp.sum(
        (
            before
            & (decode_of[None, :] == decode_of[:, None])
            & (source[None, :] == source[:, None])
        ).astype(jnp.int32),
        axis=1,
    )
    slot = jnp.sum((before & mine[None, :]).astype(jnp.int32), axis=1)
    is_late, is_last = rank >= sure, rank >= pair_share
    in_middle = mine & is_late & ~is_last
    late_rank = jnp.where(is_last, jnp.sum(in_middle.astype(jnp.int32)), 0) + jnp.sum(
        (before & ((mine & is_late)[None, :] & (is_last[None, :] == is_last[:, None]))).astype(
            jnp.int32
        ),
        axis=1,
    )
    offset = source ^ me
    first_place = offset * half_sure + rank % half_sure
    late_chunk, late_rest = late_rank // (2 * late_half), late_rank % (2 * late_half)
    late_place = late_start + late_chunk * late_half + late_rest % late_half
    side = jnp.where(is_late, late_rest // late_half, rank // half_sure) ^ parity
    place = side * half + jnp.where(is_late, late_place, first_place)
    hit = mine[None, :] & (place[None, :] == here[:, None])

    def at_place(values):
        return jnp.sum(jnp.where(hit, values[None, :], 0), axis=1)

    replicas = lax.axis_size("groups") * groups
    replica = lax.axis_index("groups") * groups + me
    slots = at_place(slot)
    lengths = at_place(kv_lengths)
    late_which = at_place(is_last.astype(jnp.int32)).reshape(2, half)[:, late_start:]
    late_index = at_place(source * late + (rank - sure) % late).reshape(2, half)[:, late_start:]
    place_of_slot = jnp.sum(
        jnp.where(mine[None, :] & (slot[None, :] == here[:, None]), place[None, :], 0), axis=1
    )

    def send_keys(own_keys, far_keys, name, *waits):
        own_keys, far_keys = held(own_keys, *waits), held(far_keys, *waits)
        return [own_keys] + [
            across(far_keys if k % 2 else own_keys, "tensor", k, name) for k in range(1, shards)
        ]

    def land(out):
        arrived = lax.all_to_all(out, "xfer", 0, 0, tiled=True)
        return arrived.reshape(groups * late, row_width, span)

    replicas = lax.axis_size("groups") * groups
    replica = lax.axis_index("groups") * groups + me

    def piece_of(weights, *waits):
        flat = weights.reshape(-1, weights.shape[-1])
        piece = cut(flat, replicas, replica, *waits)
        return across(piece, "tensor", 1, "piece")

    def between_chips(piece):
        sent = {0: piece}
        for t in range(2, replicas, 2):
            sent[t] = across(piece, ("groups", "xfer"), t, "chips")
        return sent

    def between_cores(sent):
        for t in range(0, replicas, 2):
            sent[t + 1] = across(sent[t], "xfer", 1, "cores")
        return sent

    def joined(sent, weights):
        pieces = [sent[t] for t in range(replicas)]
        return in_order(pieces, replica).reshape(weights.shape)

    def take(x, index):
        return jnp.take(x, index, axis=0, mode="clip")

    def attend_chunk(chunk, keys, waits):
        start = starts[chunk]
        live = lengths[start : start + sizes[chunk]]
        scalars = jnp.concatenate([shard[None], live]).astype(jnp.int32)
        queries = [latent_own, latent_far, rope_own, rope_far]
        return attend(scalars, start, queries, keys, new_own, steps, score_scale, waits)

    def project(latent, weights):
        size = latent.shape[0]
        out = jnp.einsum(
            "rthc,hcv->rthv",
            latent.reshape(size, steps, heads_here, latent_width),
            weights,
            preferred_element_type=jnp.float32,
        )
        return out.astype(jnp.bfloat16).reshape(size, steps, heads_here * value_width)

    def absorb(nope, weights):
        heads = nope.reshape(half, steps, heads_here, nope_width)
        latent = jnp.einsum("rthn,hnc->rthc", heads, weights, preferred_element_type=jnp.float32)
        return latent.astype(jnp.bfloat16).reshape(half, steps * heads_here, latent_width)

    def rotary(rope):
        return rope.reshape(half, steps * heads_here, rope_width)

    keys = [send_keys(*first, "keys0")]
    wk_piece = piece_of(wk_up, first[0])
    middle_in = land(held(middle_out, second[0]))
    keys.append(send_keys(*second, "keys1", *keys[0][1:], wk_piece))
    wk_sent = between_chips(held(wk_piece, *keys[0][1:]))
    wv_piece = piece_of(wv_up, *keys[0][1:])
    last_out = pack_all(values, scales, request_at(last_places), span, *keys[0][1:])
    third = select_blocks(
        [middle_in], jnp.zeros_like(late_which[:, :late_half]), late_index[:, :late_half]
    )
    keys.append(send_keys(*third, "keys2", *keys[1][1:], *list(wk_sent.values())[1:], wv_piece))
    wk_sent[0] = held(wk_sent[0], *keys[1][1:])
    for t in range(2, replicas, 2):
        wk_sent[t] = held(wk_sent[t], *keys[1][1:])
    wk_sent = between_cores(wk_sent)
    wv_sent = between_chips(held(wv_piece, *keys[1][1:]))
    last_in = land(held(last_out, *keys[1][1:]))
    nope_own, nope_far, rope_own, rope_far = by_side(
        [q_nope, q_rope], slots.reshape(2, half), *keys[1][1:]
    )
    nope_far = across(nope_far, "tensor", 1, "nope")
    rope_far = across(rope_far, "tensor", 1, "rope")
    new_own = take(new_kv, slots[:half])
    new_own = jnp.pad(new_own, ((0, 0), (0, NEW_ROWS - steps), (0, 0)))
    fourth = select_blocks(
        [middle_in, last_in], late_which[:, late_half:], late_index[:, late_half:]
    )
    before_fourth = keys[2][1:] + [wk_sent[t] for t in range(1, replicas, 2)]
    before_fourth += [wv_sent[t] for t in range(2, replicas, 2)] + [nope_far, rope_far]
    keys.append(send_keys(*fourth, "keys3", *before_fourth))
    for t in range(0, replicas, 2):
        wv_sent[t] = held(wv_sent[t], *keys[2][1:])
    wv_sent = between_cores(wv_sent)
    wk_far, wv_far = joined(wk_sent, wk_up), joined(wv_sent, wv_up)
    latent_own, latent_far = absorb(nope_own, wk_up), absorb(nope_far, wk_far)
    rope_own, rope_far = rotary(rope_own), rotary(rope_far)
    latents = []
    for chunk in range(4):
        latents.append(attend_chunk(chunk, keys[chunk], [x for x, _ in latents[-1:]]))
    far_heads = [across(project(far, wv_far), "tensor", 1, "heads") for _, far in latents]
    own_heads = [project(own, wv_up) for own, _ in latents]
    head_out = take(jnp.concatenate(own_heads + far_heads, axis=0), place_of_slot)
    partial = jnp.dot(
        head_out.reshape(per_group * steps, -1), w_out, preferred_element_type=jnp.float32
    ).astype(jnp.bfloat16)
    parts = lax.all_to_all(
        partial.reshape(shards, out_rows, steps, -1), "tensor", 0, 0, tiled=True
    )
    return jnp.sum(parts.astype(jnp.float32), axis=0).astype(jnp.bfloat16)


def solution(mesh):
    return jax.shard_map(
        local,
        mesh=mesh,
        in_specs=(
            P(("groups", "xfer", "tensor"), None),
            P(("groups", "xfer", "tensor"), None),
            P("groups"),
            P("groups"),
            P(("groups", "xfer"), None, "tensor"),
            P(("groups", "xfer"), None, "tensor"),
            P(("groups", "xfer"), None, None),
            P("tensor", None, None),
            P("tensor", None, None),
            P("tensor", None),
        ),
        out_specs=P(("groups", "xfer", "tensor"), None, None),
        check_vma=False,
    )
```

time: 542 us -> 350 us (0.65)
  waiting for transfers between devices: 310 us -> 105 us
  blocking collectives: 95.6 us -> 25.3 us
  Pallas kernels: 0 us -> 67.4 us
  starting transfers between devices: 20.2 us -> 82.5 us
  local copies, waits for them, and re-layouts: 51.3 us -> 33.5 us
  other arithmetic: 20.1 us -> 5.45 us
  between operations: 13.7 us -> 0.81 us
    all_to_all x4 -> x2, waiting for transfers between devices: 264 us -> 0.01 us  [land(): arrived = lax.all_to_all(out, 'xfer', 0, 0, tiled=True)]
    ppermute x0 -> x37, waiting for transfers between devices: none -> 105 us  [across(): lax.ppermute(x, axis, [(i, i ^ offset) for i in range(lax.axis_size(axis))])]
    ppermute x0 -> x37, starting transfers between devices: none -> 73.2 us  [across(): lax.ppermute(x, axis, [(i, i ^ offset) for i in range(lax.axis_size(axis))])]
    all_to_all x1, blocking collectives: 95.6 us -> 25.3 us  [local(): lax.all_to_all(partial.reshape(shards, out_rows, steps, -1), 'tensor', 0,...]
    pallas_call x0 -> x38, Pallas kernels: none -> 67.4 us  [the longest x4 18.5 us: attend(): pl.pallas_call(lambda *refs: attend_kernel(shards, steps, score_scale, *r...]
    psum x1 -> x0, waiting for transfers between devices: 46.1 us -> none  [local(): lax.psum(partial_sum.astype(jnp.bfloat16), 'tensor').astype(jnp.float32)]
    unnamed x16 -> x121, local copies, waits for them, and re-layouts: 0.18 us -> 17.9 us
    gather x7 -> x2, local copies, waits for them, and re-layouts: 18.2 us -> 3.3 us  [take(): return jnp.take(x, index, axis=0, mode='clip')]
  transfers between devices with their start and end apart: 5 -> 39, of which waited for: 4 -> 14; matrix products, arithmetic and copies ran while one was open for 10% -> 10% of each run, Pallas kernels for 0% -> 17%
where the time goes in v1:
time: 350 us; the launch traced here: 348 us
  waiting for transfers between devices  105 us (30%)
  starting transfers between devices  82.5 us (24%)
  Pallas kernels  67.4 us (19%)
  local copies, waits for them, and re-layouts  33.5 us (10%)
  matrix products  27.4 us (8%)
  blocking collectives  25.3 us (7%)
  other arithmetic  5.45 us (2%)
    ppermute x37, waiting for transfers between devices, across(): lax.ppermute(x, axis, [(i, i ^ offset) for i in range(lax.axis_size(axis))])  105 us
    ppermute x37, starting transfers between devices, across(): lax.ppermute(x, axis, [(i, i ^ offset) for i in range(lax.axis_size(axis))])  73.2 us
    all_to_all x1, blocking collectives, local(): lax.all_to_all(partial.reshape(shards, out_rows, steps, -1), 'tensor', 0,...  25.3 us
    pallas_call x4, Pallas kernels, attend(): pl.pallas_call(lambda *refs: attend_kernel(shards, steps, score_scale, *r...  18.5 us
    unnamed x121, local copies, waits for them, and re-layouts  17.9 us
    dot_general x1, matrix products, local(): jnp.dot(head_out.reshape(per_group * steps, -1), w_out, preferred_element...  11.6 us
    pallas_call x2, Pallas kernels, pack_all(): pl.pallas_call(kernel, grid_spec=pltpu.PrefetchScalarGridSpec(num_scalar_...  9.6 us
    dot_general x8, matrix products, project(): jnp.einsum('rthc,hcv->rthv', latent.reshape(size, steps, heads_here, late...  9.57 us
  transfers between devices with their start and end apart: 39, of which 14 were waited for; matrix products, arithmetic and copies ran while one was open for 10% of the time, Pallas kernels for 17%

profile of v1, /device:TPU:0, one launch (start us, length us, event | category | flops | bytes accessed | tf_op | source)
XLA Modules:
  0.0 347.6 jit_solution(938171669598313615)
XLA Ops:
  2.7 4.7 %shard_map.100 = (bf16[4,576,128]{2,1,0:T(8,128)(2,1)}, bf16[4,576,128]{2,1,0:T(8,128)(2,1)}, bf16[4,576,128]{2,1,0:T(8,128)(2,1)}, bf16[4,576,128]{2,1,0:T(8,128)(2,1)}) custom-call(s32[4,4]{1,0:T(4,128)} %get-tuple-element.60.refs_0_, bf16[576,4096]{1,0:T(8,128)(2,1)} %bitcast.149, bf16[576,4096]{1,0:T(8,128)(2,1)} %bitcast.150, ...), custom_call_target="tpu_custom_call" | custom-call | flops 1024 | bytes 1024 | tf_op jit(solution)/shard_map/pallas_call | solution.py:42
  19.9 4.8 %shard_map.119.refs_0_ = bf16[4,4,576,128]{3,2,1,0:T(8,128)(2,1)} custom-call(s32[4,4]{1,0:T(4,128)} %get-tuple-element.59.index_ref, bf16[576,4096]{1,0:T(8,128)(2,1)} %bitcast.153, bf16[576,4096]{1,0:T(8,128)(2,1)} %bitcast.154, bf16[576,4096]{1,0:T(8,128)(2,1)} %bitcast.155, bf16[576,4096]{1,0:T(8,128)(2,1)} %bitcast.156, bf16[4,4096]{1,0:T(4,128)(2,1)} %bitcast.166, ...), custom_call_target="tpu_custom_call" | custom-call | flops 1024 | bytes 1024 | tf_op jit(solution)/shard_map/pallas_call | solution.py:70
  26.9 3.1 collective-permute-done.1.refs_0_.refs_2_
  32.2 9.6 %collective-permute-done.2.refs_1_.refs_3_ = bf16[4,576,128]{2,1,0:T(8,128)(2,1)} collective-permute-done((bf16[4,576,128]{2,1,0:T(8,128)(2,1)}, bf16[4,576,128]{2,1,0:T(8,128)(2,1)}, u32[]{:S(2)}, u32[]{:S(2)}) %collective-permute-start.2) | collective-permute-done | bytes 589856 | tf_op jit(solution)/shard_map/early_xfer3/ppermute | solution.py:347
  44.0 4.5 %all-to-all-start = ((bf16[4,4,576,128]{3,2,1,0:T(8,128)(2,1)}), bf16[4,4,576,128]{3,2,1,0:T(8,128)(2,1)}, u32[]{:S(2)}, u32[]{:S(2)}) async-start(bf16[4,4,576,128]{3,2,1,0:T(8,128)(2,1)} %shard_map.120), calls=%async_computation | async-start | bytes 4718592 | tf_op jit(solution)/shard_map/all_to_all | solution.py:431
  49.4 18.1 %collective-permute-done.6.refs_4_.refs_0_ = bf16[512,512]{1,0:T(8,128)(2,1)S(1)} collective-permute-done((bf16[512,512]{1,0:T(8,128)(2,1)}, bf16[512,512]{1,0:T(8,128)(2,1)S(1)}, u32[]{:S(2)}, u32[]{:S(2)}) %collective-permute-start.6) | collective-permute-done | bytes 524320 | tf_op jit(solution)/shard_map/piece_tensor1/ppermute | solution.py:347
  67.6 4.3 %collective-permute-done.4.refs_2_.refs_7_.refs_1_.refs_9_ = bf16[4,576,128]{2,1,0:T(8,128)(2,1)S(1)} collective-permute-done((bf16[4,576,128]{2,1,0:T(8,128)(2,1)}, bf16[4,576,128]{2,1,0:T(8,128)(2,1)S(1)}, u32[]{:S(2)}, u32[]{:S(2)}) %collective-permute-start.4) | collective-permute-done | bytes 589856 | tf_op jit(solution)/shard_map/keys0_tensor2/ppermute | solution.py:347
  72.9 3.2 collective-permute-start.8
  84.0 16.0 %collective-permute-done.7.refs_4_.refs_1_.refs_6_ = bf16[4,576,128]{2,1,0:T(8,128)(2,1)S(1)} collective-permute-done((bf16[4,576,128]{2,1,0:T(8,128)(2,1)}, bf16[4,576,128]{2,1,0:T(8,128)(2,1)S(1)}, u32[]{:S(2)}, u32[]{:S(2)}) %collective-permute-start.7) | collective-permute-done | bytes 589856 | tf_op jit(solution)/shard_map/keys1_tensor1/ppermute | solution.py:347
  102.5 13.3 %collective-permute-done.8.refs_5_.refs_2_.refs_7_ = bf16[4,576,128]{2,1,0:T(8,128)(2,1)S(1)} collective-permute-done((bf16[4,576,128]{2,1,0:T(8,128)(2,1)}, bf16[4,576,128]{2,1,0:T(8,128)(2,1)S(1)}, u32[]{:S(2)}, u32[]{:S(2)}) %collective-permute-start.8) | collective-permute-done | bytes 589856 | tf_op jit(solution)/shard_map/keys1_tensor2/ppermute | solution.py:347
  117.5 9.3 %shard_map.110 = (bf16[16,4,4096]{2,1,0:T(4,128)(2,1)}, bf16[16,4,4096]{2,1,0:T(4,128)(2,1)}, bf16[16,4,2048]{2,1,0:T(4,128)(2,1)}, bf16[16,4,2048]{2,1,0:T(4,128)(2,1)}) custom-call(s32[2,16]{1,0:T(2,128)} %reshape.365.index_ref, bf16[32,4,4096]{2,1,0:T(4,128)(2,1)} %refs_1_.1, bf16[32,4,4096]{2,1,0:T(4,128)(2,1)} %refs_1_.1, bf16[32,4,2048]{2,1,0:T(4,128)(2,1)} %refs_3_.1, ...), custom_call_target="tpu_custom_call" | custom-call | flops 1024 | bytes 1024 | tf_op jit(solution)/shard_map/pallas_call | solution.py:217
  126.8 11.0 %collective-permute-start.18 = (bf16[16,4,2048]{2,1,0:T(4,128)(2,1)}, bf16[16,4,2048]{2,1,0:T(4,128)(2,1)S(1)}, u32[]{:S(2)}, u32[]{:S(2)}) collective-permute-start(bf16[16,4,2048]{2,1,0:T(4,128)(2,1)} %get-tuple-element.40), channel_id=1, source_target_pairs={{0,1},{1,0},{2,3},{3,2},{4,5},{5,4},{6,7},{7,6},{8,9},{9,8},{10,11... | collective-permute-start | bytes 786440 | tf_op jit(solution)/shard_map/rope_tensor1/ppermute | solution.py:347
  139.4 4.2 %shard_map.121 = (bf16[4,576,128]{2,1,0:T(8,128)(2,1)}, bf16[4,576,128]{2,1,0:T(8,128)(2,1)}) custom-call(s32[2,4]{1,0:T(2,128)} %broadcast_10_which_ref.2.which_ref, s32[2,4]{1,0:T(2,128)} %get-tuple-element.65.index_ref, bf16[16,576,128]{2,1,0:T(8,128)(2,1)} %bitcast.22.refs_0_.refs_1_.refs_2_, bf16[16,576,128]{2,1,0:T(8,128)(2,1)} %bitcast.22.refs_0_.refs_1_.refs_2_), custom_call_target="tpu_custom_call" | custom-call | flops 1024 | bytes 1024 | tf_op jit(solution)/shard_map/pallas_call | solution.py:147
  147.8 4.8 %shard_map.126.refs_0_ = bf16[4,4,576,128]{3,2,1,0:T(8,128)(2,1)} custom-call(s32[4,4]{1,0:T(4,128)} %get-tuple-element.58.index_ref, bf16[576,4096]{1,0:T(8,128)(2,1)} %bitcast.157, bf16[576,4096]{1,0:T(8,128)(2,1)} %bitcast.158, bf16[576,4096]{1,0:T(8,128)(2,1)} %bitcast.159, bf16[576,4096]{1,0:T(8,128)(2,1)} %bitcast.160, bf16[4,4096]{1,0:T(4,128)(2,1)} %bitcast.170, ...), custom_call_target="tpu_custom_call" | custom-call | flops 1024 | bytes 1024 | tf_op jit(solution)/shard_map/pallas_call | solution.py:70
  153.1 3.0 convert_bitcast_fusion.1
  158.6 4.8 %all-to-all-start.1 = ((bf16[4,4,576,128]{3,2,1,0:T(8,128)(2,1)}), bf16[4,4,576,128]{3,2,1,0:T(8,128)(2,1)}, u32[]{:S(2)}, u32[]{:S(2)}) async-start(bf16[4,4,576,128]{3,2,1,0:T(8,128)(2,1)} %shard_map.127), calls=%async_computation.1 | async-start | bytes 4718592 | tf_op jit(solution)/shard_map/all_to_all | solution.py:431
  174.9 4.2 %shard_map.116 = bf16[8,512,512]{2,1,0:T(8,128)(2,1)} custom-call(s32[1]{0:T(128)} %bitcast.6.which_ref.replica_ref, bf16[512,512]{1,0:T(8,128)(2,1)} %shard_map.112.refs_0_, bf16[512,512]{1,0:T(8,128)(2,1)} %collective-permute-done.10.refs_1_.refs_4_, bf16[512,512]{1,0:T(8,128)(2,1)} %shard_map.113.refs_2_, ...), custom_call_target="tpu_custom_call" | custom-call | flops 1024 | bytes 1024 | tf_op jit(solution)/shard_map/pallas_call | solution.py:175
  179.2 3.2 convert_bitcast_fusion
  183.7 4.0 %shard_map.117 = (bf16[4,128,512]{2,1,0:T(8,128)(2,1)S(1)}, bf16[4,128,512]{2,1,0:T(8,128)(2,1)S(1)}) custom-call(s32[5]{0:T(128)S(1)} %pad_add_fusion.refs_0_, bf16[16,128,512]{2,1,0:T(8,128)(2,1)S(1)} %bitcast.126, bf16[16,128,512]{2,1,0:T(8,128)(2,1)S(1)} %bitcast.130, bf16[16,128,64]{2,1,0:T(8,128)(2,1)S(1)} %copy-done.20, ...), custom_call_target="tpu_custom_call" | custom-call | flops 1024 | bytes 1024 | tf_op jit(solution)/shard_map/pallas_call | solution.py:300
  189.4 4.0 %shard_map.118 = (bf16[4,128,512]{2,1,0:T(8,128)(2,1)S(1)}, bf16[4,128,512]{2,1,0:T(8,128)(2,1)S(1)}) custom-call(s32[5]{0:T(128)S(1)} %pad_add_fusion.1.refs_0_, bf16[16,128,512]{2,1,0:T(8,128)(2,1)S(1)} %bitcast.127, bf16[16,128,512]{2,1,0:T(8,128)(2,1)S(1)} %bitcast.131, bf16[16,128,64]{2,1,0:T(8,128)(2,1)S(1)} %copy-done.20, ...), custom_call_target="tpu_custom_call" | custom-call | flops 1024 | bytes 1024 | tf_op jit(solution)/shard_map/pallas_call | solution.py:300
  198.5 4.4 %shard_map.128 = (bf16[4,576,128]{2,1,0:T(8,128)(2,1)}, bf16[4,576,128]{2,1,0:T(8,128)(2,1)}) custom-call(s32[2,4]{1,0:T(2,128)} %slice.35.which_ref, s32[2,4]{1,0:T(2,128)} %get-tuple-element.64.index_ref, bf16[16,576,128]{2,1,0:T(8,128)(2,1)} %bitcast.22.refs_0_.refs_1_.refs_2_, bf16[16,576,128]{2,1,0:T(8,128)(2,1)} %bitcast.26.refs_1_.refs_3_, ...), custom_call_target="tpu_custom_call" | custom-call | flops 1024 | bytes 1024 | tf_op jit(solution)/shard_map/pallas_call | solution.py:147
  202.9 8.9 %collective-permute-done.21.refs_7_.refs_2_ = bf16[4,576,128]{2,1,0:T(8,128)(2,1)S(1)} collective-permute-done((bf16[4,576,128]{2,1,0:T(8,128)(2,1)}, bf16[4,576,128]{2,1,0:T(8,128)(2,1)S(1)}, u32[]{:S(2)}, u32[]{:S(2)}) %collective-permute-start.21) | collective-permute-done | bytes 589856 | tf_op jit(solution)/shard_map/keys2_tensor2/ppermute | solution.py:347
  218.8 5.2 %shard_map.125 = (bf16[4,128,512]{2,1,0:T(8,128)(2,1)S(1)}, bf16[4,128,512]{2,1,0:T(8,128)(2,1)S(1)}) custom-call(s32[5]{0:T(128)S(1)} %pad_add_fusion.2.refs_0_, bf16[16,128,512]{2,1,0:T(8,128)(2,1)S(1)} %bitcast.128, bf16[16,128,512]{2,1,0:T(8,128)(2,1)S(1)} %bitcast.132, bf16[16,128,64]{2,1,0:T(8,128)(2,1)S(1)} %copy-done.21, ...), custom_call_target="tpu_custom_call" | custom-call | flops 1024 | bytes 1024 | tf_op jit(solution)/shard_map/pallas_call | solution.py:300
  225.8 12.2 %collective-permute-start.26 = (bf16[4,576,128]{2,1,0:T(8,128)(2,1)}, bf16[4,576,128]{2,1,0:T(8,128)(2,1)S(1)}, u32[]{:S(2)}, u32[]{:S(2)}) collective-permute-start(bf16[4,576,128]{2,1,0:T(8,128)(2,1)} %shard_map.131), channel_id=1, source_target_pairs={{0,1},{1,0},{2,3},{3,2},{4,5},{5,4},{6,7},{7,6},{8,9},{9,8},{10,11... | collective-permute-start | bytes 1769480 | tf_op jit(solution)/shard_map/keys3_tensor1/ppermute | solution.py:347
  243.3 4.2 %shard_map.137 = bf16[8,2048,128]{2,1,0:T(8,128)(2,1)} custom-call(s32[1]{0:T(128)} %bitcast.6.which_ref.replica_ref, bf16[2048,128]{1,0:T(8,128)(2,1)} %shard_map.133.refs_0_, bf16[2048,128]{1,0:T(8,128)(2,1)} %collective-permute-done.29.refs_1_, bf16[2048,128]{1,0:T(8,128)(2,1)} %shard_map.134.refs_2_, bf16[2048,128]{1,0:T(8,128)(2,1)} %collective-permute-done.30.refs_3_, ...), custom_call_target="tpu_custom_call" | custom-call | flops 1024 | bytes 1024 | tf_op jit(solution)/shard_map/pallas_call | solution.py:175
  247.5 3.3 fusion.24
  255.1 6.4 %collective-permute-done.26.refs_6_ = bf16[4,576,128]{2,1,0:T(8,128)(2,1)S(1)} collective-permute-done((bf16[4,576,128]{2,1,0:T(8,128)(2,1)}, bf16[4,576,128]{2,1,0:T(8,128)(2,1)S(1)}, u32[]{:S(2)}, u32[]{:S(2)}) %collective-permute-start.26) | collective-permute-done | bytes 589856 | tf_op jit(solution)/shard_map/keys3_tensor1/ppermute | solution.py:347
  261.5 21.3 %collective-permute-done.27.refs_7_ = bf16[4,576,128]{2,1,0:T(8,128)(2,1)} collective-permute-done((bf16[4,576,128]{2,1,0:T(8,128)(2,1)S(1)}, bf16[4,576,128]{2,1,0:T(8,128)(2,1)}, u32[]{:S(2)}, u32[]{:S(2)}) %collective-permute-start.27) | collective-permute-done | bytes 589856 | tf_op jit(solution)/shard_map/keys3_tensor2/ppermute | solution.py:347
  282.8 5.4 %shard_map.132 = (bf16[4,128,512]{2,1,0:T(8,128)(2,1)S(1)}, bf16[4,128,512]{2,1,0:T(8,128)(2,1)S(1)}) custom-call(s32[5]{0:T(128)S(1)} %pad_add_fusion.3.refs_0_, bf16[16,128,512]{2,1,0:T(8,128)(2,1)S(1)} %bitcast.129, bf16[16,128,512]{2,1,0:T(8,128)(2,1)S(1)} %bitcast.133, bf16[16,128,64]{2,1,0:T(8,128)(2,1)S(1)} %copy-done.22, ...), custom_call_target="tpu_custom_call" | custom-call | flops 1024 | bytes 1024 | tf_op jit(solution)/shard_map/pallas_call | solution.py:300
  290.1 12.5 %collective-permute-start.36 = (bf16[4,4,4096]{2,1,0:T(4,128)(2,1)S(1)}, bf16[4,4,4096]{2,1,0:T(4,128)(2,1)S(1)}, u32[]{:S(2)}, u32[]{:S(2)}) collective-permute-start(bf16[4,4,4096]{2,1,0:T(4,128)(2,1)S(1)} %bitcast.185), channel_id=1, source_target_pairs={{0,1},{1,0},{2,3},{3,2},{4,5},{5,4},{6,7},{7,6},{8,9},{9,8},{10,11... | collective-permute-start | bytes 393224 | tf_op jit(solution)/shard_map/heads_tensor1/ppermute | solution.py:347
  309.2 11.6 %convolution_convert_fusion = bf16[128,3584]{1,0:T(8,128)(2,1)S(1)} fusion(bf16[128,4096]{1,0:T(8,128)(2,1)S(1)} %reshape.400, bf16[4096,3584]{1,0:T(8,128)(2,1)} %param.19), kind=kOutput, calls=%fused_computation.2 | convolution fusion | flops 3758555136 | bytes 31326208 | tf_op jit(solution)/shard_map/dot_general | solution.py:527
  321.0 25.3 %all_to_all.15 = bf16[4,8,4,3584]{3,2,1,0:T(4,128)(2,1)S(1)} all-to-all(bf16[4,8,4,3584]{3,2,1,0:T(4,128)(2,1)S(1)} %reshape.401), channel_id=1, replica_groups=mesh['groups'=2,'xfer'=4,'tensor'=4] {'tensor'}, dimensions={0} | all-to-all | bytes 1835008 | tf_op jit(solution)/shard_map/all_to_all | solution.py:530
  (262 shorter events, 91.8 us)
Async XLA Ops:
  15.7 26.1 %collective-permute-start.2 = (bf16[4,576,128]{2,1,0:T(8,128)(2,1)}, bf16[4,576,128]{2,1,0:T(8,128)(2,1)}, u32[]{:S(2)}, u32[]{:S(2)}) collective-permute-start(bf16[4,576,128]{2,1,0:T(8,128)(2,1)} %shard_map.103), channel_id=1, source_target_pairs={{0,12},{4,8},{8,4},{12,0},{1,13},{5,9},{9,5},{13,1},{2,14},{6,10},... | collective-permute-start | bytes 1769480 | tf_op jit(solution)/shard_map/early_xfer3/ppermute | solution.py:347
  15.7 51.9 %collective-permute-start.3 = (bf16[4,576,128]{2,1,0:T(8,128)(2,1)}, bf16[4,576,128]{2,1,0:T(8,128)(2,1)S(1)}, u32[]{:S(2)}, u32[]{:S(2)}) collective-permute-start(bf16[4,576,128]{2,1,0:T(8,128)(2,1)} %shard_map.105), channel_id=1, source_target_pairs={{0,1},{1,0},{2,3},{3,2},{4,5},{5,4},{6,7},{7,6},{8,9},{9,8},{10,11... | collective-permute-start | bytes 1769480 | tf_op jit(solution)/shard_map/keys0_tensor1/ppermute | solution.py:347
  17.4 54.5 %collective-permute-start.5 = (bf16[4,576,128]{2,1,0:T(8,128)(2,1)}, bf16[4,576,128]{2,1,0:T(8,128)(2,1)S(1)}, u32[]{:S(2)}, u32[]{:S(2)}) collective-permute-start(bf16[4,576,128]{2,1,0:T(8,128)(2,1)} %shard_map.105), channel_id=1, source_target_pairs={{0,3},{1,2},{2,1},{3,0},{4,7},{5,6},{6,5},{7,4},{8,11},{9,10},{10,... | collective-permute-start | bytes 1769480 | tf_op jit(solution)/shard_map/keys0_tensor3/ppermute | solution.py:347
  26.6 45.3 %collective-permute-start.4 = (bf16[4,576,128]{2,1,0:T(8,128)(2,1)}, bf16[4,576,128]{2,1,0:T(8,128)(2,1)S(1)}, u32[]{:S(2)}, u32[]{:S(2)}) collective-permute-start(bf16[4,576,128]{2,1,0:T(8,128)(2,1)} %shard_map.106.refs_5_), channel_id=1, source_target_pairs={{0,2},{1,3},{2,0},{3,1},{4,6},{5,7},{6,4},{7,5},{8,10},{9,11},{10,... | collective-permute-start | bytes 1769480 | tf_op jit(solution)/shard_map/keys0_tensor2/ppermute | solution.py:347
  30.0 37.5 %collective-permute-start.6 = (bf16[512,512]{1,0:T(8,128)(2,1)}, bf16[512,512]{1,0:T(8,128)(2,1)S(1)}, u32[]{:S(2)}, u32[]{:S(2)}) collective-permute-start(bf16[512,512]{1,0:T(8,128)(2,1)} %shard_map.107), channel_id=1, source_target_pairs={{0,1},{1,0},{2,3},{3,2},{4,5},{5,4},{6,7},{7,6},{8,9},{9,8},{10,11... | collective-permute-start | bytes 1572872 | tf_op jit(solution)/shard_map/piece_tensor1/ppermute | solution.py:347
  44.0 94.8 %all-to-all-start = ((bf16[4,4,576,128]{3,2,1,0:T(8,128)(2,1)}), bf16[4,4,576,128]{3,2,1,0:T(8,128)(2,1)}, u32[]{:S(2)}, u32[]{:S(2)}) async-start(bf16[4,4,576,128]{3,2,1,0:T(8,128)(2,1)} %shard_map.120), calls=%async_computation | async-start | bytes 4718592 | tf_op jit(solution)/shard_map/all_to_all | solution.py:431
  72.9 27.0 %collective-permute-start.7 = (bf16[4,576,128]{2,1,0:T(8,128)(2,1)}, bf16[4,576,128]{2,1,0:T(8,128)(2,1)S(1)}, u32[]{:S(2)}, u32[]{:S(2)}) collective-permute-start(bf16[4,576,128]{2,1,0:T(8,128)(2,1)} %shard_map.108), channel_id=1, source_target_pairs={{0,1},{1,0},{2,3},{3,2},{4,5},{5,4},{6,7},{7,6},{8,9},{9,8},{10,11... | collective-permute-start | bytes 1769480 | tf_op jit(solution)/shard_map/keys1_tensor1/ppermute | solution.py:347
  72.9 42.9 %collective-permute-start.8 = (bf16[4,576,128]{2,1,0:T(8,128)(2,1)}, bf16[4,576,128]{2,1,0:T(8,128)(2,1)S(1)}, u32[]{:S(2)}, u32[]{:S(2)}) collective-permute-start(bf16[4,576,128]{2,1,0:T(8,128)(2,1)} %shard_map.109.refs_5_), channel_id=1, source_target_pairs={{0,2},{1,3},{2,0},{3,1},{4,6},{5,7},{6,4},{7,5},{8,10},{9,11},{10,... | collective-permute-start | bytes 1769480 | tf_op jit(solution)/shard_map/keys1_tensor2/ppermute | solution.py:347
  76.7 39.2 %collective-permute-start.9 = (bf16[4,576,128]{2,1,0:T(8,128)(2,1)}, bf16[4,576,128]{2,1,0:T(8,128)(2,1)S(1)}, u32[]{:S(2)}, u32[]{:S(2)}) collective-permute-start(bf16[4,576,128]{2,1,0:T(8,128)(2,1)} %shard_map.108), channel_id=1, source_target_pairs={{0,3},{1,2},{2,1},{3,0},{4,7},{5,6},{6,5},{7,4},{8,11},{9,10},{10,... | collective-permute-start | bytes 1769480 | tf_op jit(solution)/shard_map/keys1_tensor3/ppermute | solution.py:347
  79.0 59.6 %collective-permute-start.11 = (bf16[512,512]{1,0:T(8,128)(2,1)}, bf16[512,512]{1,0:T(8,128)(2,1)}, u32[]{:S(2)}, u32[]{:S(2)}) collective-permute-start(bf16[512,512]{1,0:T(8,128)(2,1)} %shard_map.111.refs_0_), channel_id=1, source_target_pairs={{0,8},{4,12},{8,0},{12,4},{16,24},{20,28},{24,16},{28,20},{1,9},{5... | collective-permute-start | bytes 1572872 | tf_op jit(solution)/shard_map/chips_both2/ppermute | solution.py:347
  80.6 58.1 %collective-permute-start.13 = (bf16[512,512]{1,0:T(8,128)(2,1)}, bf16[512,512]{1,0:T(8,128)(2,1)S(1)}, u32[]{:S(2)}, u32[]{:S(2)}) collective-permute-start(bf16[512,512]{1,0:T(8,128)(2,1)} %shard_map.111.refs_0_), channel_id=1, source_target_pairs={{0,16},{4,20},{8,24},{12,28},{16,0},{20,4},{24,8},{28,12},{1,17},{... | collective-permute-start | bytes 1572872 | tf_op jit(solution)/shard_map/chips_both4/ppermute | solution.py:347
  99.9 38.7 %collective-permute-start.15 = (bf16[512,512]{1,0:T(8,128)(2,1)S(1)}, bf16[512,512]{1,0:T(8,128)(2,1)}, u32[]{:S(2)}, u32[]{:S(2)}) collective-permute-start(bf16[512,512]{1,0:T(8,128)(2,1)S(1)} %copy-done.42), channel_id=1, source_target_pairs={{0,24},{4,28},{8,16},{12,20},{16,8},{20,12},{24,0},{28,4},{1,25},{... | collective-permute-start | bytes 1572872 | tf_op jit(solution)/shard_map/chips_both6/ppermute | solution.py:347
  115.9 27.8 %collective-permute-start.19 = (bf16[2048,128]{1,0:T(8,128)(2,1)}, bf16[2048,128]{1,0:T(8,128)(2,1)}, u32[]{:S(2)}, u32[]{:S(2)}) collective-permute-start(bf16[2048,128]{1,0:T(8,128)(2,1)} %shard_map.122), channel_id=1, source_target_pairs={{0,1},{1,0},{2,3},{3,2},{4,5},{5,4},{6,7},{7,6},{8,9},{9,8},{10,11... | collective-permute-start | bytes 1572872 | tf_op jit(solution)/shard_map/piece_tensor1/ppermute | solution.py:347
  126.8 18.1 %collective-permute-start.18 = (bf16[16,4,2048]{2,1,0:T(4,128)(2,1)}, bf16[16,4,2048]{2,1,0:T(4,128)(2,1)S(1)}, u32[]{:S(2)}, u32[]{:S(2)}) collective-permute-start(bf16[16,4,2048]{2,1,0:T(4,128)(2,1)} %get-tuple-element.40), channel_id=1, source_target_pairs={{0,1},{1,0},{2,3},{3,2},{4,5},{5,4},{6,7},{7,6},{8,9},{9,8},{10,11... | collective-permute-start | bytes 786440 | tf_op jit(solution)/shard_map/rope_tensor1/ppermute | solution.py:347
  138.7 30.6 %collective-permute-start.10 = (bf16[512,512]{1,0:T(8,128)(2,1)}, bf16[512,512]{1,0:T(8,128)(2,1)}, u32[]{:S(2)}, u32[]{:S(2)}) collective-permute-start(bf16[512,512]{1,0:T(8,128)(2,1)} %shard_map.112.refs_0_), channel_id=1, source_target_pairs={{0,4},{4,0},{8,12},{12,8},{1,5},{5,1},{9,13},{13,9},{2,6},{6,2},{1... | collective-permute-start | bytes 1572872 | tf_op jit(solution)/shard_map/cores_xfer1/ppermute | solution.py:347
  138.8 25.9 %collective-permute-start.17 = (bf16[16,4,4096]{2,1,0:T(4,128)(2,1)}, bf16[16,4,4096]{2,1,0:T(4,128)(2,1)S(1)}, u32[]{:S(2)}, u32[]{:S(2)}) collective-permute-start(bf16[16,4,4096]{2,1,0:T(4,128)(2,1)} %get-tuple-element.38), channel_id=1, source_target_pairs={{0,1},{1,0},{2,3},{3,2},{4,5},{5,4},{6,7},{7,6},{8,9},{9,8},{10,11... | collective-permute-start | bytes 1572872 | tf_op jit(solution)/shard_map/nope_tensor1/ppermute | solution.py:347
  143.7 26.4 %collective-permute-start.12 = (bf16[512,512]{1,0:T(8,128)(2,1)}, bf16[512,512]{1,0:T(8,128)(2,1)}, u32[]{:S(2)}, u32[]{:S(2)}) collective-permute-start(bf16[512,512]{1,0:T(8,128)(2,1)} %shard_map.113.refs_2_), channel_id=1, source_target_pairs={{0,4},{4,0},{8,12},{12,8},{1,5},{5,1},{9,13},{13,9},{2,6},{6,2},{1... | collective-permute-start | bytes 1572872 | tf_op jit(solution)/shard_map/cores_xfer1/ppermute | solution.py:347
  144.2 27.4 %collective-permute-start.14 = (bf16[512,512]{1,0:T(8,128)(2,1)}, bf16[512,512]{1,0:T(8,128)(2,1)}, u32[]{:S(2)}, u32[]{:S(2)}) collective-permute-start(bf16[512,512]{1,0:T(8,128)(2,1)} %shard_map.114.refs_4_), channel_id=1, source_target_pairs={{0,4},{4,0},{8,12},{12,8},{1,5},{5,1},{9,13},{13,9},{2,6},{6,2},{1... | collective-permute-start | bytes 1572872 | tf_op jit(solution)/shard_map/cores_xfer1/ppermute | solution.py:347
  144.9 28.5 %collective-permute-start.16 = (bf16[512,512]{1,0:T(8,128)(2,1)}, bf16[512,512]{1,0:T(8,128)(2,1)}, u32[]{:S(2)}, u32[]{:S(2)}) collective-permute-start(bf16[512,512]{1,0:T(8,128)(2,1)} %shard_map.115.refs_6_), channel_id=1, source_target_pairs={{0,4},{4,0},{8,12},{12,8},{1,5},{5,1},{9,13},{13,9},{2,6},{6,2},{1... | collective-permute-start | bytes 1572872 | tf_op jit(solution)/shard_map/cores_xfer1/ppermute | solution.py:347
  158.6 39.9 %all-to-all-start.1 = ((bf16[4,4,576,128]{3,2,1,0:T(8,128)(2,1)}), bf16[4,4,576,128]{3,2,1,0:T(8,128)(2,1)}, u32[]{:S(2)}, u32[]{:S(2)}) async-start(bf16[4,4,576,128]{3,2,1,0:T(8,128)(2,1)} %shard_map.127), calls=%async_computation.1 | async-start | bytes 4718592 | tf_op jit(solution)/shard_map/all_to_all | solution.py:431
  166.8 28.4 %collective-permute-start.20 = (bf16[4,576,128]{2,1,0:T(8,128)(2,1)}, bf16[4,576,128]{2,1,0:T(8,128)(2,1)S(1)}, u32[]{:S(2)}, u32[]{:S(2)}) collective-permute-start(bf16[4,576,128]{2,1,0:T(8,128)(2,1)} %shard_map.124), channel_id=1, source_target_pairs={{0,1},{1,0},{2,3},{3,2},{4,5},{5,4},{6,7},{7,6},{8,9},{9,8},{10,11... | collective-permute-start | bytes 1769480 | tf_op jit(solution)/shard_map/keys2_tensor1/ppermute | solution.py:347
  169.2 42.6 %collective-permute-start.21 = (bf16[4,576,128]{2,1,0:T(8,128)(2,1)}, bf16[4,576,128]{2,1,0:T(8,128)(2,1)S(1)}, u32[]{:S(2)}, u32[]{:S(2)}) collective-permute-start(bf16[4,576,128]{2,1,0:T(8,128)(2,1)} %shard_map.123.refs_5_), channel_id=1, source_target_pairs={{0,2},{1,3},{2,0},{3,1},{4,6},{5,7},{6,4},{7,5},{8,10},{9,11},{10,... | collective-permute-start | bytes 1769480 | tf_op jit(solution)/shard_map/keys2_tensor2/ppermute | solution.py:347
  170.1 41.8 %collective-permute-start.22 = (bf16[4,576,128]{2,1,0:T(8,128)(2,1)}, bf16[4,576,128]{2,1,0:T(8,128)(2,1)}, u32[]{:S(2)}, u32[]{:S(2)}) collective-permute-start(bf16[4,576,128]{2,1,0:T(8,128)(2,1)} %shard_map.124), channel_id=1, source_target_pairs={{0,3},{1,2},{2,1},{3,0},{4,7},{5,6},{6,5},{7,4},{8,11},{9,10},{10,... | collective-permute-start | bytes 1769480 | tf_op jit(solution)/shard_map/keys2_tensor3/ppermute | solution.py:347
  171.6 54.2 %collective-permute-start.23 = (bf16[2048,128]{1,0:T(8,128)(2,1)}, bf16[2048,128]{1,0:T(8,128)(2,1)}, u32[]{:S(2)}, u32[]{:S(2)}) collective-permute-start(bf16[2048,128]{1,0:T(8,128)(2,1)} %shard_map.129.refs_0_), channel_id=1, source_target_pairs={{0,8},{4,12},{8,0},{12,4},{16,24},{20,28},{24,16},{28,20},{1,9},{5... | collective-permute-start | bytes 1572872 | tf_op jit(solution)/shard_map/chips_both2/ppermute | solution.py:347
  173.4 52.4 %collective-permute-start.24 = (bf16[2048,128]{1,0:T(8,128)(2,1)}, bf16[2048,128]{1,0:T(8,128)(2,1)}, u32[]{:S(2)}, u32[]{:S(2)}) collective-permute-start(bf16[2048,128]{1,0:T(8,128)(2,1)} %shard_map.129.refs_0_), channel_id=1, source_target_pairs={{0,16},{4,20},{8,24},{12,28},{16,0},{20,4},{24,8},{28,12},{1,17},{... | collective-permute-start | bytes 1572872 | tf_op jit(solution)/shard_map/chips_both4/ppermute | solution.py:347
  195.2 30.6 %collective-permute-start.25 = (bf16[2048,128]{1,0:T(8,128)(2,1)}, bf16[2048,128]{1,0:T(8,128)(2,1)}, u32[]{:S(2)}, u32[]{:S(2)}) collective-permute-start(bf16[2048,128]{1,0:T(8,128)(2,1)} %shard_map.129.refs_0_), channel_id=1, source_target_pairs={{0,24},{4,28},{8,16},{12,20},{16,8},{20,12},{24,0},{28,4},{1,25},{... | collective-permute-start | bytes 1572872 | tf_op jit(solution)/shard_map/chips_both6/ppermute | solution.py:347
  225.8 35.7 %collective-permute-start.26 = (bf16[4,576,128]{2,1,0:T(8,128)(2,1)}, bf16[4,576,128]{2,1,0:T(8,128)(2,1)S(1)}, u32[]{:S(2)}, u32[]{:S(2)}) collective-permute-start(bf16[4,576,128]{2,1,0:T(8,128)(2,1)} %shard_map.131), channel_id=1, source_target_pairs={{0,1},{1,0},{2,3},{3,2},{4,5},{5,4},{6,7},{7,6},{8,9},{9,8},{10,11... | collective-permute-start | bytes 1769480 | tf_op jit(solution)/shard_map/keys3_tensor1/ppermute | solution.py:347
  240.3 42.5 %collective-permute-start.27 = (bf16[4,576,128]{2,1,0:T(8,128)(2,1)S(1)}, bf16[4,576,128]{2,1,0:T(8,128)(2,1)}, u32[]{:S(2)}, u32[]{:S(2)}) collective-permute-start(bf16[4,576,128]{2,1,0:T(8,128)(2,1)S(1)} %copy-done.30), channel_id=1, source_target_pairs={{0,2},{1,3},{2,0},{3,1},{4,6},{5,7},{6,4},{7,5},{8,10},{9,11},{10,... | collective-permute-start | bytes 1769480 | tf_op jit(solution)/shard_map/keys3_tensor2/ppermute | solution.py:347
  241.2 41.6 %collective-permute-start.28 = (bf16[4,576,128]{2,1,0:T(8,128)(2,1)}, bf16[4,576,128]{2,1,0:T(8,128)(2,1)}, u32[]{:S(2)}, u32[]{:S(2)}) collective-permute-start(bf16[4,576,128]{2,1,0:T(8,128)(2,1)} %shard_map.131), channel_id=1, source_target_pairs={{0,3},{1,2},{2,1},{3,0},{4,7},{5,6},{6,5},{7,4},{8,11},{9,10},{10,... | collective-permute-start | bytes 1769480 | tf_op jit(solution)/shard_map/keys3_tensor3/ppermute | solution.py:347
  250.9 52.3 %collective-permute-start.33 = (bf16[4,4,4096]{2,1,0:T(4,128)(2,1)S(1)}, bf16[4,4,4096]{2,1,0:T(4,128)(2,1)S(1)}, u32[]{:S(2)}, u32[]{:S(2)}) collective-permute-start(bf16[4,4,4096]{2,1,0:T(4,128)(2,1)S(1)} %bitcast.182), channel_id=1, source_target_pairs={{0,1},{1,0},{2,3},{3,2},{4,5},{5,4},{6,7},{7,6},{8,9},{9,8},{10,11... | collective-permute-start | bytes 393224 | tf_op jit(solution)/shard_map/heads_tensor1/ppermute | solution.py:347
  252.5 51.5 %collective-permute-start.34 = (bf16[4,4,4096]{2,1,0:T(4,128)(2,1)S(1)}, bf16[4,4,4096]{2,1,0:T(4,128)(2,1)S(1)}, u32[]{:S(2)}, u32[]{:S(2)}) collective-permute-start(bf16[4,4,4096]{2,1,0:T(4,128)(2,1)S(1)} %bitcast.183), channel_id=1, source_target_pairs={{0,1},{1,0},{2,3},{3,2},{4,5},{5,4},{6,7},{7,6},{8,9},{9,8},{10,11... | collective-permute-start | bytes 393224 | tf_op jit(solution)/shard_map/heads_tensor1/ppermute | solution.py:347
  261.5 43.2 %collective-permute-start.35 = (bf16[4,4,4096]{2,1,0:T(4,128)(2,1)S(1)}, bf16[4,4,4096]{2,1,0:T(4,128)(2,1)S(1)}, u32[]{:S(2)}, u32[]{:S(2)}) collective-permute-start(bf16[4,4,4096]{2,1,0:T(4,128)(2,1)S(1)} %bitcast.184), channel_id=1, source_target_pairs={{0,1},{1,0},{2,3},{3,2},{4,5},{5,4},{6,7},{7,6},{8,9},{9,8},{10,11... | collective-permute-start | bytes 393224 | tf_op jit(solution)/shard_map/heads_tensor1/ppermute | solution.py:347
  (64 other events, 635.3 us)

commit v2 on v1

--- a/solution.py
+++ b/solution.py
@@ -84,18 +84,19 @@
     )(index, *([values] * groups), *([scales] * groups), *waits)
 
 
-def held(x, *waits):
+def held(arrays, *waits):
     def kernel(*refs):
         pass
 
     anywhere = pl.BlockSpec(memory_space=pl.ANY)
     return pl.pallas_call(
         kernel,
-        in_specs=[anywhere] * (1 + len(waits)),
-        out_specs=anywhere,
-        out_shape=jax.ShapeDtypeStruct(x.shape, x.dtype),
-        input_output_aliases={0: 0},
-    )(x, *waits)
+        in_specs=[anywhere] * (len(arrays) + len(waits)),
+        out_specs=[anywhere] * len(arrays),
+        out_shape=[jax.ShapeDtypeStruct(x.shape, x.dtype) for x in arrays],
+        input_output_aliases={i: i for i in range(len(arrays))},
+        cost_estimate=SHORT,
+    )(*arrays, *waits)
 
 
 def regroup_kernel(count, *refs):
@@ -123,9 +124,37 @@
     return tuple(x.reshape(count * half, width, span) for x in outs)
 
 
-def select_kernel(which_ref, index_ref, *refs):
+def regroup_arrived(arrived, offsets, me):
+    rows, width, span = arrived.shape[1:]
+    half, count = rows // 2, len(offsets)
+
+    def spec(offset, first):
+        return pl.BlockSpec(
+            (1, 1, width, span), lambda n, me_ref: (me_ref[0] ^ offset, first + n, 0, 0)
+        )
+
+    def kernel(me_ref, *refs):
+        for side in range(2):
+            for k in range(count):
+                refs[2 * count + side][k, 0] = refs[side * count + k][0, 0]
+
+    outs = pl.pallas_call(
+        kernel,
+        grid_spec=pltpu.PrefetchScalarGridSpec(
+            num_scalar_prefetch=1,
+            grid=(half,),
+            in_specs=[spec(k, 0) for k in offsets] + [spec(k, half) for k in offsets],
+            out_specs=[pl.BlockSpec((count, 1, width, span), lambda n, me_ref: (0, n, 0, 0))] * 2,
+        ),
+        out_shape=[jax.ShapeDtypeStruct((count, half, width, span), jnp.bfloat16)] * 2,
+        cost_estimate=SHORT,
+    )(me[None], *([arrived] * (2 * count)))
+    return tuple(x.reshape(count * half, width, span) for x in outs)
+
+
+def select_kernel(sources, which_ref, index_ref, *refs):
     n = pl.program_id(0)
-    sources = (len(refs) - 2) // 2
+    refs = refs[: 2 * sources] + refs[-2:]
     for side in range(2):
         for source in range(sources):
 
@@ -134,7 +163,7 @@
                 refs[2 * sources + side][...] = refs[side * sources + source][...]
 
 
-def select_blocks(arrived, which, index):
+def select_blocks(arrived, which, index, *waits):
     count = index.shape[1]
     width, span = arrived[0].shape[1:]
 
@@ -145,95 +174,185 @@
         return pl.BlockSpec((1, width, span), place)
 
     return pl.pallas_call(
-        select_kernel,
+        lambda *refs: select_kernel(len(arrived), *refs),
         grid_spec=pltpu.PrefetchScalarGridSpec(
             num_scalar_prefetch=2,
             grid=(count,),
-            in_specs=[pick(i, j) for i in range(2) for j in range(len(arrived))],
+            in_specs=[pick(i, j) for i in range(2) for j in range(len(arrived))]
+            + [pl.BlockSpec(memory_space=pl.ANY)] * len(waits),
             out_specs=[pl.BlockSpec((1, width, span), lambda n, *refs: (n, 0, 0))] * 2,
         ),
         out_shape=[jax.ShapeDtypeStruct((count, width, span), jnp.bfloat16)] * 2,
         cost_estimate=SHORT,
-    )(which, index, *arrived, *arrived)
-
-
-def in_order(pieces, replica):
-    count, shape = len(pieces), pieces[0].shape
-
-    def kernel(replica_ref, *refs):
-        out_ref, done = refs[count], refs[count + 1]
-        copies = [
-            pltpu.make_async_copy(refs[t], out_ref.at[replica_ref[0] ^ t], done.at[t])
-            for t in range(count)
-        ]
-        for copy in copies:
-            copy.start()
-        for copy in copies:
-            copy.wait()
-
-    anywhere = pl.BlockSpec(memory_space=pl.ANY)
-    return pl.pallas_call(
-        kernel,
-        in_specs=[pl.BlockSpec(memory_space=pltpu.SMEM)] + [anywhere] * count,
-        out_specs=pl.BlockSpec(memory_space=pltpu.VMEM),
-        out_shape=jax.ShapeDtypeStruct((count,) + shape, pieces[0].dtype),
-        scratch_shapes=[pltpu.SemaphoreType.DMA((count,))],
-        cost_estimate=SHORT,
-    )(replica[None], *pieces)
-
-
-def cut(flat, pieces, which, *waits):
-    rows, columns = flat.shape[0] // pieces, flat.shape[1]
-
-    def kernel(which_ref, flat_ref, *refs):
-        refs[-1][...] = flat_ref[...]
+    )(which, index, *arrived, *arrived, *waits)
+
+
+def cut(wk, wv, pieces, which, *waits):
+    width, narrow = wk.shape[1], wv.shape[1]
+    rows, folds = wk.shape[0] // pieces, width // narrow
+
+    def kernel(which_ref, wk_ref, wv_ref, *refs):
+        refs[-1][:rows, :] = wk_ref[...]
+        for fold in range(folds):
+            columns = slice(fold * narrow, (fold + 1) * narrow)
+            refs[-1][rows:, columns] = wv_ref[fold * rows : (fold + 1) * rows, :]
+
+    def block(rows, columns):
+        return pl.BlockSpec((rows, columns), lambda n, which_ref: (which_ref[0], 0))
 
     return pl.pallas_call(
         kernel,
         grid_spec=pltpu.PrefetchScalarGridSpec(
             num_scalar_prefetch=1,
             grid=(1,),
-            in_specs=[pl.BlockSpec((rows, columns), lambda n, which_ref: (which_ref[0], 0))]
+            in_specs=[block(rows, width), block(folds * rows, narrow)]
             + [pl.BlockSpec(memory_space=pl.ANY)] * len(waits),
-            out_specs=pl.BlockSpec((rows, columns), lambda n, which_ref: (0, 0)),
-        ),
-        out_shape=jax.ShapeDtypeStruct((rows, columns), flat.dtype),
-        cost_estimate=SHORT,
-    )(which[None], flat, *waits)
+            out_specs=pl.BlockSpec((2 * rows, width), lambda n, which_ref: (0, 0)),
+        ),
+        out_shape=jax.ShapeDtypeStruct((2 * rows, width), wk.dtype),
+        cost_estimate=SHORT,
+    )(which[None], wk, wv, *waits)
+
+
+def doubled(near, far):
+    count, rows, width = near.shape
+
+    def kernel(near_ref, far_ref, out_ref):
+        out_ref[0] = near_ref[...]
+        out_ref[1] = far_ref[...]
+
+    spec = pl.BlockSpec((1, rows, width), lambda n: (n, 0, 0))
+    out = pl.pallas_call(
+        kernel,
+        grid=(count,),
+        in_specs=[spec] * 2,
+        out_specs=pl.BlockSpec((2, 1, rows, width), lambda n: (0, n, 0, 0)),
+        out_shape=jax.ShapeDtypeStruct((2, count, rows, width), near.dtype),
+        cost_estimate=SHORT,
+    )(near, far)
+    return out.reshape(2 * count, rows, width)
+
+
+def in_order(near, far, replica, narrow, *waits):
+    count, rows, width = near.shape
+    rows, folds = rows // 2, width // narrow
+
+    def pick(n, replica_ref):
+        return (n ^ replica_ref[0]) // 2, 0, 0
+
+    def kernel(replica_ref, near_ref, far_ref, *refs):
+        wk_out, wv_out = refs[-2:]
+        odd = (pl.program_id(0) ^ replica_ref[0]) & 1
+
+        def put(source):
+            wk_out[0] = source[0, :rows, :]
+            for fold in range(folds):
+                columns = slice(fold * narrow, (fold + 1) * narrow)
+                wv_out[0, fold * rows : (fold + 1) * rows, :] = source[0, rows:, columns]
+
+        @pl.when(odd == 0)
+        def _():
+            put(near_ref)
+
+        @pl.when(odd == 1)
+        def _():
+            put(far_ref)
+
+    return pl.pallas_call(
+        kernel,
+        grid_spec=pltpu.PrefetchScalarGridSpec(
+            num_scalar_prefetch=1,
+            grid=(2 * count,),
+            in_specs=[pl.BlockSpec((1, 2 * rows, width), pick)] * 2
+            + [pl.BlockSpec(memory_space=pl.ANY)] * len(waits),
+            out_specs=[
+                pl.BlockSpec((1, rows, width), lambda n, replica_ref: (n, 0, 0)),
+                pl.BlockSpec((1, folds * rows, narrow), lambda n, replica_ref: (n, 0, 0)),
+            ],
+        ),
+        out_shape=[
+            jax.ShapeDtypeStruct((2 * count, rows, width), near.dtype),
+            jax.ShapeDtypeStruct((2 * count, folds * rows, narrow), near.dtype),
+        ],
+        cost_estimate=SHORT,
+    )(replica[None], near, far, *waits)
 
 
 def by_side(arrays, index, *waits):
     count = index.shape[1]
-
-    def pick(side, x):
-        return pl.BlockSpec(
-            (1,) + x.shape[1:], lambda n, index_ref: (index_ref[side, n], 0, 0)
-        )
+    steps = arrays[0].shape[1]
+    width = sum(x.shape[2] for x in arrays)
 
     def kernel(index_ref, *refs):
-        for i in range(2 * len(arrays)):
-            refs[i - 2 * len(arrays)][...] = refs[i][...]
-
-    return pl.pallas_call(
-        kernel,
-        grid_spec=pltpu.PrefetchScalarGridSpec(
-            num_scalar_prefetch=1,
-            grid=(count,),
-            in_specs=[pick(side, x) for x in arrays for side in range(2)]
-            + [pl.BlockSpec(memory_space=pl.ANY)] * len(waits),
-            out_specs=[
-                pl.BlockSpec((1,) + x.shape[1:], lambda n, index_ref: (n, 0, 0))
-                for x in arrays
-                for side in range(2)
-            ],
-        ),
+        outs, staged = refs[-3:-1], refs[-1]
+        for side in range(2):
+            first = 0
+            for x_ref in refs[: len(arrays)]:
+                columns = slice(first, first + x_ref.shape[2])
+                first += x_ref.shape[2]
+                for n in range(count):
+                    rows = x_ref[index_ref[side, n]].astype(jnp.float32)
+                    staged[n * steps : (n + 1) * steps, columns] = rows
+            outs[side][...] = staged[...].astype(outs[side].dtype)
+
+    vmem = pl.BlockSpec(memory_space=pltpu.VMEM)
+    return pl.pallas_call(
+        kernel,
+        in_specs=[pl.BlockSpec(memory_space=pltpu.SMEM)]
+        + [vmem] * len(arrays)
+        + [pl.BlockSpec(memory_space=pl.ANY)] * len(waits),
+        out_specs=[vmem] * 2,
+        out_shape=[jax.ShapeDtypeStruct((count * steps, width), arrays[0].dtype)] * 2,
+        scratch_shapes=[pltpu.VMEM((count * steps, width), jnp.float32)],
+        compiler_params=pltpu.CompilerParams(vmem_limit_bytes=24 * 1024 * 1024),
+        cost_estimate=SHORT,
+    )(index, *arrays, *waits)
+
+
+def absorb(queries, weights, steps, *waits):
+    rows = queries.shape[0]
+    heads, nope_width, latent_width = weights.shape
+    rope_width = queries.shape[1] // heads - nope_width
+
+    def kernel(queries_ref, weights_ref, *refs):
+        latent_out, rope_out, latent_rows, rope_rows = refs[len(waits) :]
+        for head in range(heads):
+            place = pl.ds(head, rows, stride=heads)
+            columns = slice(head * nope_width, (head + 1) * nope_width)
+            product = jnp.dot(
+                queries_ref[:, columns], weights_ref[head], preferred_element_type=jnp.float32
+            )
+            for block in range(latent_width // 128):
+                latent_rows[block, place, :] = product[:, block * 128 : (block + 1) * 128]
+            first = heads * nope_width + head * rope_width
+            part = queries_ref[:, first : first + rope_width].astype(jnp.float32)
+            rope_rows[place, :] = jnp.concatenate([part] * (128 // rope_width), axis=1)
+        for block in range(latent_width // 128):
+            columns = slice(block * 128, (block + 1) * 128)
+            latent_out[:, columns] = latent_rows[block].astype(jnp.bfloat16)
+        rope_out[...] = rope_rows[:, :rope_width].astype(jnp.bfloat16)
+
+    vmem = pl.BlockSpec(memory_space=pltpu.VMEM)
+    latent, rotary = pl.pallas_call(
+        kernel,
+        in_specs=[vmem] * 2 + [pl.BlockSpec(memory_space=pl.ANY)] * len(waits),
+        out_specs=[vmem] * 2,
         out_shape=[
-            jax.ShapeDtypeStruct((count,) + x.shape[1:], x.dtype)
-            for x in arrays
-            for side in range(2)
+            jax.ShapeDtypeStruct((rows * heads, latent_width), jnp.bfloat16),
+            jax.ShapeDtypeStruct((rows * heads, rope_width), jnp.bfloat16),
         ],
-        cost_estimate=SHORT,
-    )(index, *[x for x in arrays for side in range(2)], *waits)
+        scratch_shapes=[
+            pltpu.VMEM((latent_width // 128, rows * heads, 128), jnp.float32),
+            pltpu.VMEM((rows * heads, 128), jnp.float32),
+        ],
+        compiler_params=pltpu.CompilerParams(vmem_limit_bytes=24 * 1024 * 1024),
+        cost_estimate=SHORT,
+    )(queries, weights, *waits)
+    slots = rows // steps
+    return (
+        latent.reshape(slots, steps * heads, latent_width),
+        rotary.reshape(slots, steps * heads, rope_width),
+    )
 
 
 def attend_kernel(shards, steps, score_scale, scalars, *refs):
@@ -313,6 +432,51 @@
         compiler_params=pltpu.CompilerParams(vmem_limit_bytes=32 * 1024 * 1024),
         cost_estimate=SHORT,
     )(scalars, *queries, *keys, new_rows, *waits)
+
+
+def output(head_out, row_of, w_out, shards):
+    rows, columns = row_of.shape[0], w_out.shape[1]
+    depth, width = w_out.shape[0], 512
+    while columns % width:
+        width //= 2
+
+    def kernel(row_ref, *refs):
+        heads, w_ref = refs[: len(head_out)], refs[len(head_out)]
+        outs, ordered = refs[len(head_out) + 1 : -1], refs[-1]
+
+        @pl.when(pl.program_id(0) == 0)
+        def _():
+            place = lax.broadcasted_iota(jnp.int32, (rows, rows), 1)
+            chosen = (place == row_ref[...]).astype(jnp.bfloat16)
+            stacked = jnp.concatenate([ref[...] for ref in heads], axis=0)
+            ordered[...] = jnp.dot(
+                chosen, stacked, preferred_element_type=jnp.float32
+            ).astype(jnp.bfloat16)
+
+        result = jnp.dot(ordered[...], w_ref[...], preferred_element_type=jnp.float32)
+        share = rows // shards
+        for k in range(shards):
+            outs[k][...] = result[k * share : (k + 1) * share].astype(jnp.bfloat16)
+
+    def whole(x):
+        return pl.BlockSpec(x.shape, lambda n: (0, 0))
+
+    return pl.pallas_call(
+        kernel,
+        grid=(columns // width,),
+        in_specs=[whole(row_of)]
+        + [whole(x) for x in head_out]
+        + [pl.BlockSpec((depth, width), lambda n: (0, n))],
+        out_specs=[pl.BlockSpec((rows // shards, width), lambda n: (0, n))] * shards,
+        out_shape=[jax.ShapeDtypeStruct((rows // shards, columns), jnp.bfloat16)] * shards,
+        scratch_shapes=[pltpu.VMEM((rows, depth), jnp.bfloat16)],
+        compiler_params=pltpu.CompilerParams(vmem_limit_bytes=30 * 1024 * 1024),
+        cost_estimate=pl.CostEstimate(
+            flops=2 * rows * depth * columns,
+            bytes_accessed=2 * depth * columns,
+            transcendentals=0,
+        ),
+    )(row_of, *head_out, w_out)
 
 
 def local(kv_values, kv_scales, decode_of, kv_lengths, q_nope, q_rope, new_kv, wk_up, wv_up, w_out):
@@ -372,12 +536,10 @@
     else:
         values = kv_values.reshape(per_group, span, -1).swapaxes(1, 2)
         scales = kv_scales.reshape(per_group, span, -1).swapaxes(1, 2)
-    early = pack(values, scales, request_at(early_places), span)
-    first = regroup([early[0], across(early[1], "xfer", 1, "early")])
-    middle_out = pack_all(values, scales, request_at(middle_places), span, first[0])
-    second = regroup(
-        [across(held(early[k], first[0]), "xfer", k, "early") for k in range(2, groups)]
-    )
+    near = pack(values, scales, request_at(early_places[:2]), span)
+    first = regroup([near[0], across(near[1], "xfer", 1, "early")])
+    far_places = offsets[:, None] * pair_room + early_ranks[None, :]
+    early_out = pack_all(values, scales, request_at(far_places), span, first[0])
 
     ids = jnp.arange(requests, dtype=jnp.int32)
     source = ids // per_group
@@ -421,38 +583,24 @@
         jnp.where(mine[None, :] & (slot[None, :] == here[:, None]), place[None, :], 0), axis=1
     )
 
-    def send_keys(own_keys, far_keys, name, *waits):
-        own_keys, far_keys = held(own_keys, *waits), held(far_keys, *waits)
-        return [own_keys] + [
+    def send_keys(chunk, name, waits=(), carried=()):
+        if waits:
+            own_keys, far_keys, *carried = held([*chunk, *carried], *waits)
+        else:
+            own_keys, far_keys = chunk
+        keys = [own_keys] + [
             across(far_keys if k % 2 else own_keys, "tensor", k, name) for k in range(1, shards)
         ]
+        return keys, *carried
 
     def land(out):
-        arrived = lax.all_to_all(out, "xfer", 0, 0, tiled=True)
+        return lax.all_to_all(out, "xfer", 0, 0, tiled=True)
+
+    def flat(arrived):
         return arrived.reshape(groups * late, row_width, span)
 
     replicas = lax.axis_size("groups") * groups
     replica = lax.axis_index("groups") * groups + me
-
-    def piece_of(weights, *waits):
-        flat = weights.reshape(-1, weights.shape[-1])
-        piece = cut(flat, replicas, replica, *waits)
-        return across(piece, "tensor", 1, "piece")
-
-    def between_chips(piece):
-        sent = {0: piece}
-        for t in range(2, replicas, 2):
-            sent[t] = across(piece, ("groups", "xfer"), t, "chips")
-        return sent
-
-    def between_cores(sent):
-        for t in range(0, replicas, 2):
-            sent[t + 1] = across(sent[t], "xfer", 1, "cores")
-        return sent
-
-    def joined(sent, weights):
-        pieces = [sent[t] for t in range(replicas)]
-        return in_order(pieces, replica).reshape(weights.shape)
 
     def take(x, index):
         return jnp.take(x, index, axis=0, mode="clip")
@@ -474,63 +622,58 @@
         )
         return out.astype(jnp.bfloat16).reshape(size, steps, heads_here * value_width)
 
-    def absorb(nope, weights):
-        heads = nope.reshape(half, steps, heads_here, nope_width)
-        latent = jnp.einsum("rthn,hnc->rthc", heads, weights, preferred_element_type=jnp.float32)
-        return latent.astype(jnp.bfloat16).reshape(half, steps * heads_here, latent_width)
-
-    def rotary(rope):
-        return rope.reshape(half, steps * heads_here, rope_width)
-
-    keys = [send_keys(*first, "keys0")]
-    wk_piece = piece_of(wk_up, first[0])
-    middle_in = land(held(middle_out, second[0]))
-    keys.append(send_keys(*second, "keys1", *keys[0][1:], wk_piece))
-    wk_sent = between_chips(held(wk_piece, *keys[0][1:]))
-    wv_piece = piece_of(wv_up, *keys[0][1:])
+    wk, wv = (x.reshape(-1, x.shape[-1]) for x in (wk_up, wv_up))
+    hops = [("xfer", 1 << i) for i in range(1, groups.bit_length() - 1)]
+    hops += [("groups", 1 << i) for i in range((replicas // groups).bit_length() - 1)]
+    keys = list(send_keys(first, "keys0"))
+    stack = across(cut(wk, wv, replicas, replica, first[0]), "tensor", 1, "weights")[None]
+    second = regroup_arrived(land(early_out), range(2, groups), me)
+    sent, stack = send_keys(second, "keys1", keys[0][1:], [stack])
+    keys.append(sent)
+    queries_own, queries_far = by_side([q_nope, q_rope], slots.reshape(2, half), *keys[0][1:])
+    queries_far = across(queries_far, "tensor", 1, "queries")
+    middle_out = pack_all(values, scales, request_at(middle_places), span, second[0])
+    middle_in = flat(land(middle_out))
     last_out = pack_all(values, scales, request_at(last_places), span, *keys[0][1:])
+    for axis, offset in hops[:-1]:
+        stack = doubled(stack, across(stack, axis, offset, "weights"))
     third = select_blocks(
         [middle_in], jnp.zeros_like(late_which[:, :late_half]), late_index[:, :late_half]
     )
-    keys.append(send_keys(*third, "keys2", *keys[1][1:], *list(wk_sent.values())[1:], wv_piece))
-    wk_sent[0] = held(wk_sent[0], *keys[1][1:])
-    for t in range(2, replicas, 2):
-        wk_sent[t] = held(wk_sent[t], *keys[1][1:])
-    wk_sent = between_cores(wk_sent)
-    wv_sent = between_chips(held(wv_piece, *keys[1][1:]))
-    last_in = land(held(last_out, *keys[1][1:]))
-    nope_own, nope_far, rope_own, rope_far = by_side(
-        [q_nope, q_rope], slots.reshape(2, half), *keys[1][1:]
-    )
-    nope_far = across(nope_far, "tensor", 1, "nope")
-    rope_far = across(rope_far, "tensor", 1, "rope")
+    latent_own, rope_own = absorb(queries_own, wk_up, steps, third[0])
+    sent, stack = send_keys(third, "keys2", [*keys[1][1:], queries_far, latent_own, last_out], [stack])
+    keys.append(sent)
+    last_in = flat(land(last_out))
+    for axis, offset in hops[-1:]:
+        stack = doubled(stack, across(stack, axis, offset, "weights"))
+    fourth = select_blocks(
+        [middle_in, last_in], late_which[:, late_half:], late_index[:, late_half:]
+    )
+    sent, stack = send_keys(fourth, "keys3", keys[2][1:], [stack])
+    keys.append(sent)
+    wk_far, wv_far = in_order(stack, across(stack, "xfer", 1, "weights"), replica, wv.shape[-1])
+    wk_far, wv_far = wk_far.reshape(wk_up.shape), wv_far.reshape(wv_up.shape)
+    latent_far, rope_far = absorb(queries_far, wk_far, steps)
     new_own = take(new_kv, slots[:half])
     new_own = jnp.pad(new_own, ((0, 0), (0, NEW_ROWS - steps), (0, 0)))
-    fourth = select_blocks(
-        [middle_in, last_in], late_which[:, late_half:], late_index[:, late_half:]
-    )
-    before_fourth = keys[2][1:] + [wk_sent[t] for t in range(1, replicas, 2)]
-    before_fourth += [wv_sent[t] for t in range(2, replicas, 2)] + [nope_far, rope_far]
-    keys.append(send_keys(*fourth, "keys3", *before_fourth))
-    for t in range(0, replicas, 2):
-        wv_sent[t] = held(wv_sent[t], *keys[2][1:])
-    wv_sent = between_cores(wv_sent)
-    wk_far, wv_far = joined(wk_sent, wk_up), joined(wv_sent, wv_up)
-    latent_own, latent_far = absorb(nope_own, wk_up), absorb(nope_far, wk_far)
-    rope_own, rope_far = rotary(rope_own), rotary(rope_far)
-    latents = []
+    latents, own_heads, far_heads = [], [], []
     for chunk in range(4):
-        latents.append(attend_chunk(chunk, keys[chunk], [x for x, _ in latents[-1:]]))
-    far_heads = [across(project(far, wv_far), "tensor", 1, "heads") for _, far in latents]
-    own_heads = [project(own, wv_up) for own, _ in latents]
-    head_out = take(jnp.concatenate(own_heads + far_heads, axis=0), place_of_slot)
-    partial = jnp.dot(
-        head_out.reshape(per_group * steps, -1), w_out, preferred_element_type=jnp.float32
-    ).astype(jnp.bfloat16)
-    parts = lax.all_to_all(
-        partial.reshape(shards, out_rows, steps, -1), "tensor", 0, 0, tiled=True
-    )
-    return jnp.sum(parts.astype(jnp.float32), axis=0).astype(jnp.bfloat16)
+        waits = [x for x, _ in latents[-1:]] if chunk < 3 else own_heads + far_heads
+        own, far = attend_chunk(chunk, keys[chunk], waits)
+        latents.append((own, far))
+        far_heads.append(project(far, wv_far))
+        own_heads.append(project(own, wv_up))
+    far_heads = [across(x, "tensor", 1, "heads") for x in far_heads]
+    head_out = [x.reshape(-1, x.shape[-1]) for x in own_heads + far_heads]
+    row = jnp.arange(per_group * steps, dtype=jnp.int32)
+    slot_of_row = ((shard ^ (row // (out_rows * steps))) * out_rows * steps) + row % (
+        out_rows * steps
+    )
+    row_of = jnp.take(place_of_slot, slot_of_row // steps, mode="clip") * steps + row % steps
+    parts = output(head_out, row_of[:, None], w_out, shards)
+    parts = [parts[0]] + [across(parts[k], "tensor", k, "output") for k in range(1, shards)]
+    summed = sum(x.astype(jnp.float32) for x in parts).astype(jnp.bfloat16)
+    return summed.reshape(out_rows, steps, -1)
 
 
 def solution(mesh):

time: 350 us -> 324 us (0.926)
  Pallas kernels: 67.4 us -> 96.6 us
  waiting for transfers between devices: 105 us -> 131 us
  blocking collectives: 25.3 us -> 0 us
  starting transfers between devices: 82.5 us -> 57.5 us
  matrix products: 27.4 us -> 7.04 us
  local copies, waits for them, and re-layouts: 33.5 us -> 23.9 us
    all_to_all x2 -> x3, waiting for transfers between devices: 0.01 us -> 42.9 us  [land(): return lax.all_to_all(out, 'xfer', 0, 0, tiled=True)]
    ppermute x37 -> x25, starting transfers between devices: 73.2 us -> 43.7 us  [across(): lax.ppermute(x, axis, [(i, i ^ offset) for i in range(lax.axis_size(axis))])]
    pallas_call x27 -> x13, Pallas kernels: 26.4 us -> 54.1 us  [the longest x1 12.6 us: output(): pl.pallas_call(kernel, grid=(columns // width,), in_specs=[whole(row_of)]...]
    all_to_all x1 -> x0, blocking collectives: 25.3 us -> none  [local(): lax.all_to_all(partial.reshape(shards, out_rows, steps, -1), 'tensor', 0,...]
    dot_general x3 -> x0, matrix products: 17.8 us -> none  [the longest x1 11.6 us: local(): jnp.dot(head_out.reshape(per_group * steps, -1), w_out, preferred_element...]
    ppermute x37 -> x25, waiting for transfers between devices: 105 us -> 87.7 us  [across(): lax.ppermute(x, axis, [(i, i ^ offset) for i in range(lax.axis_size(axis))])]
    all_to_all x2 -> x3, starting transfers between devices: 9.35 us -> 13.8 us  [land(): return lax.all_to_all(out, 'xfer', 0, 0, tiled=True)]
    pallas_call x2 -> x3, Pallas kernels: 9.6 us -> 13.8 us  [pack_all(): pl.pallas_call(kernel, grid_spec=pltpu.PrefetchScalarGridSpec(num_scalar_...]
  transfers between devices with their start and end apart: 39 -> 28, of which waited for: 14 -> 13; matrix products, arithmetic and copies ran while one was open for 10% -> 5% of each run, Pallas kernels for 17% -> 23%
where the time goes in v2:
time: 324 us; the launch traced here: 322 us
  waiting for transfers between devices  131 us (40%)
  Pallas kernels  96.6 us (30%)
  starting transfers between devices  57.5 us (18%)
  local copies, waits for them, and re-layouts  23.9 us (7%)
  matrix products  7.04 us (2%)
  other arithmetic  5.27 us (2%)
    ppermute x25, waiting for transfers between devices, across(): lax.ppermute(x, axis, [(i, i ^ offset) for i in range(lax.axis_size(axis))])  87.7 us
    ppermute x25, starting transfers between devices, across(): lax.ppermute(x, axis, [(i, i ^ offset) for i in range(lax.axis_size(axis))])  43.7 us
    all_to_all x3, waiting for transfers between devices, land(): return lax.all_to_all(out, 'xfer', 0, 0, tiled=True)  42.9 us
    pallas_call x4, Pallas kernels, attend(): pl.pallas_call(lambda *refs: attend_kernel(shards, steps, score_scale, *r...  19.9 us
    unnamed x80, local copies, waits for them, and re-layouts  17.6 us
    all_to_all x3, starting transfers between devices, land(): return lax.all_to_all(out, 'xfer', 0, 0, tiled=True)  13.8 us
    pallas_call x3, Pallas kernels, pack_all(): pl.pallas_call(kernel, grid_spec=pltpu.PrefetchScalarGridSpec(num_scalar_...  13.8 us
    pallas_call x1, Pallas kernels, output(): pl.pallas_call(kernel, grid=(columns // width,), in_specs=[whole(row_of)]...  12.6 us
  transfers between devices with their start and end apart: 28, of which 13 were waited for; matrix products, arithmetic and copies ran while one was open for 5% of the time, Pallas kernels for 23%

profile of v2, /device:TPU:0, one launch (start us, length us, event | category | flops | bytes accessed | tf_op | source)
XLA Modules:
  0.0 321.5 jit_solution(11032186587997770492)
XLA Ops:
  2.5 4.2 %shard_map.100 = (bf16[4,576,128]{2,1,0:T(8,128)(2,1)}, bf16[4,576,128]{2,1,0:T(8,128)(2,1)}) custom-call(s32[2,4]{1,0:T(2,128)} %select_reduce_fusion.8.refs_0_, bf16[576,4096]{1,0:T(8,128)(2,1)} %bitcast.173, bf16[576,4096]{1,0:T(8,128)(2,1)} %bitcast.174, bf16[4,4096]{1,0:T(4,128)(2,1)} %bitcast.189, bf16[4,4096]{1,0:T(4,128)(2,1)} %bitcast.190), custom_call_target="tpu_custom_call" | custom-call | flops 1024 | bytes 1024 | tf_op jit(solution)/shard_map/pallas_call | solution.py:42
  12.1 4.8 %shard_map.103 = bf16[4,4,576,128]{3,2,1,0:T(8,128)(2,1)} custom-call(s32[4,4]{1,0:T(4,128)} %get-tuple-element.91.index_ref, bf16[576,4096]{1,0:T(8,128)(2,1)} %bitcast.175, bf16[576,4096]{1,0:T(8,128)(2,1)} %bitcast.176, bf16[576,4096]{1,0:T(8,128)(2,1)} %bitcast.177, bf16[576,4096]{1,0:T(8,128)(2,1)} %bitcast.178, bf16[4,4096]{1,0:T(4,128)(2,1)} %bitcast.191, ...), custom_call_target="tpu_custom_call" | custom-call | flops 1024 | bytes 1024 | tf_op jit(solution)/shard_map/pallas_call | solution.py:70
  17.0 4.5 %all-to-all-start = ((bf16[4,4,576,128]{3,2,1,0:T(8,128)(2,1)}), bf16[4,4,576,128]{3,2,1,0:T(8,128)(2,1)}, u32[]{:S(2)}, u32[]{:S(2)}) async-start(bf16[4,4,576,128]{3,2,1,0:T(8,128)(2,1)} %shard_map.103), calls=%async_computation | async-start | bytes 4718592 | tf_op jit(solution)/shard_map/all_to_all | solution.py:597
  31.2 19.6 %all-to-all-done.refs_0_.refs_1_.refs_2_.refs_3_ = bf16[4,4,576,128]{3,2,1,0:T(8,128)(2,1)} async-done(((bf16[4,4,576,128]{3,2,1,0:T(8,128)(2,1)}), bf16[4,4,576,128]{3,2,1,0:T(8,128)(2,1)}, u32[]{:S(2)}, u32[]{:S(2)}) %all-to-all-start) | async-done | bytes 2359328 | tf_op jit(solution)/shard_map/all_to_all | solution.py:597
  53.1 4.8 %shard_map.105 = bf16[4,4,576,128]{3,2,1,0:T(8,128)(2,1)} custom-call(s32[4,4]{1,0:T(4,128)} %get-tuple-element.92.index_ref, bf16[576,4096]{1,0:T(8,128)(2,1)} %bitcast.179, bf16[576,4096]{1,0:T(8,128)(2,1)} %bitcast.180, bf16[576,4096]{1,0:T(8,128)(2,1)} %bitcast.181, bf16[576,4096]{1,0:T(8,128)(2,1)} %bitcast.182, bf16[4,4096]{1,0:T(4,128)(2,1)} %bitcast.195, ...), custom_call_target="tpu_custom_call" | custom-call | flops 1024 | bytes 1024 | tf_op jit(solution)/shard_map/pallas_call | solution.py:70
  58.0 4.6 %all-to-all-start.1 = ((bf16[4,4,576,128]{3,2,1,0:T(8,128)(2,1)}), bf16[4,4,576,128]{3,2,1,0:T(8,128)(2,1)}, u32[]{:S(2)}, u32[]{:S(2)}) async-start(bf16[4,4,576,128]{3,2,1,0:T(8,128)(2,1)} %shard_map.105), calls=%async_computation.1 | async-start | bytes 4718592 | tf_op jit(solution)/shard_map/all_to_all | solution.py:597
  63.7 12.4 %collective-permute-done.1.refs_2_.refs_8_.refs_3_.refs_6_ = bf16[4,576,128]{2,1,0:T(8,128)(2,1)S(1)} collective-permute-done((bf16[4,576,128]{2,1,0:T(8,128)(2,1)}, bf16[4,576,128]{2,1,0:T(8,128)(2,1)S(1)}, u32[]{:S(2)}, u32[]{:S(2)}) %collective-permute-start.1) | collective-permute-done | bytes 589856 | tf_op jit(solution)/shard_map/keys0_tensor1/ppermute | solution.py:511
  76.1 14.9 %collective-permute-done.3.refs_4_.refs_10_.refs_5_.refs_8_ = bf16[4,576,128]{2,1,0:T(8,128)(2,1)S(1)} collective-permute-done((bf16[4,576,128]{2,1,0:T(8,128)(2,1)}, bf16[4,576,128]{2,1,0:T(8,128)(2,1)S(1)}, u32[]{:S(2)}, u32[]{:S(2)}) %collective-permute-start.3) | collective-permute-done | bytes 589856 | tf_op jit(solution)/shard_map/keys0_tensor3/ppermute | solution.py:511
  106.9 4.1 %shard_map.108.refs_8_ = bf16[4,4,576,128]{3,2,1,0:T(8,128)(2,1)} custom-call(s32[4,4]{1,0:T(4,128)} %get-tuple-element.90.index_ref, bf16[576,4096]{1,0:T(8,128)(2,1)} %bitcast.183, bf16[576,4096]{1,0:T(8,128)(2,1)} %bitcast.184, bf16[576,4096]{1,0:T(8,128)(2,1)} %bitcast.185, bf16[576,4096]{1,0:T(8,128)(2,1)} %bitcast.186, bf16[4,4096]{1,0:T(4,128)(2,1)} %bitcast.199, ...), custom_call_target="tpu_custom_call" | custom-call | flops 1024 | bytes 1024 | tf_op jit(solution)/shard_map/pallas_call | solution.py:70
  111.0 5.8 %collective-permute-done.6.far_ref = bf16[1,1024,512]{2,1,0:T(8,128)(2,1)} collective-permute-done((bf16[1,1024,512]{2,1,0:T(8,128)(2,1)}, bf16[1,1024,512]{2,1,0:T(8,128)(2,1)}, u32[]{:S(2)}, u32[]{:S(2)}) %collective-permute-start.6) | collective-permute-done | bytes 1048608 | tf_op jit(solution)/shard_map/weights_xfer2/ppermute | solution.py:511
  116.8 3.0 shard_map.112
  120.4 4.3 %shard_map.106 = (bf16[4,576,128]{2,1,0:T(8,128)(2,1)}, bf16[4,576,128]{2,1,0:T(8,128)(2,1)}) custom-call(s32[2,4]{1,0:T(2,128)} %broadcast_10_refs_0_.2.refs_0_, s32[2,4]{1,0:T(2,128)} %get-tuple-element.97.refs_1_, bf16[16,576,128]{2,1,0:T(8,128)(2,1)} %bitcast.7.refs_2_.refs_3_.refs_4_, bf16[16,576,128]{2,1,0:T(8,128)(2,1)} %bitcast.7.refs_2_.refs_3_.refs_4_), custom_call_target="tpu_custom_call" | custom-call | flops 1024 | bytes 1024 | tf_op jit(solution)/shard_map/pallas_call | solution.py:176
  129.0 5.8 %shard_map.107 = (bf16[2048,512]{1,0:T(8,128)(2,1)S(1)}, bf16[2048,64]{1,0:T(8,128)(2,1)S(1)}) custom-call(bf16[64,6144]{1,0:T(8,128)(2,1)S(1)} %copy-done.30, bf16[32,128,512]{2,1,0:T(8,128)(2,1)S(1)} %copy-done.4, bf16[4,576,128]{2,1,0:T(8,128)(2,1)S(1)} %copy-done.16), custom_call_target="tpu_custom_call" | custom-call | flops 1024 | bytes 1024 | tf_op jit(solution)/shard_map/pallas_call | solution.py:336
  136.1 22.2 %collective-permute-done.7.refs_3_.refs_6_ = bf16[4,576,128]{2,1,0:T(8,128)(2,1)S(1)} collective-permute-done((bf16[4,576,128]{2,1,0:T(8,128)(2,1)}, bf16[4,576,128]{2,1,0:T(8,128)(2,1)S(1)}, u32[]{:S(2)}, u32[]{:S(2)}) %collective-permute-start.7) | collective-permute-done | bytes 589856 | tf_op jit(solution)/shard_map/keys1_tensor1/ppermute | solution.py:511
  160.9 4.7 %all-to-all-start.2 = ((bf16[4,4,576,128]{3,2,1,0:T(8,128)(2,1)}), bf16[4,4,576,128]{3,2,1,0:T(8,128)(2,1)}, u32[]{:S(2)}, u32[]{:S(2)}) async-start(bf16[4,4,576,128]{3,2,1,0:T(8,128)(2,1)} %shard_map.108.refs_8_), calls=%async_computation.2 | async-start | bytes 4718592 | tf_op jit(solution)/shard_map/all_to_all | solution.py:597
  170.8 23.2 %all-to-all-done.2 = bf16[4,4,576,128]{3,2,1,0:T(8,128)(2,1)} async-done(((bf16[4,4,576,128]{3,2,1,0:T(8,128)(2,1)}), bf16[4,4,576,128]{3,2,1,0:T(8,128)(2,1)}, u32[]{:S(2)}, u32[]{:S(2)}) %all-to-all-start.2) | async-done | bytes 2359328 | tf_op jit(solution)/shard_map/all_to_all | solution.py:597
  194.0 4.4 %shard_map.109 = (bf16[4,576,128]{2,1,0:T(8,128)(2,1)}, bf16[4,576,128]{2,1,0:T(8,128)(2,1)}) custom-call(s32[2,4]{1,0:T(2,128)} %slice.35.refs_0_, s32[2,4]{1,0:T(2,128)} %get-tuple-element.96.refs_1_, bf16[16,576,128]{2,1,0:T(8,128)(2,1)} %bitcast.7.refs_2_.refs_3_.refs_4_, bf16[16,576,128]{2,1,0:T(8,128)(2,1)} %bitcast.10.refs_3_.refs_5_, ...), custom_call_target="tpu_custom_call" | custom-call | flops 1024 | bytes 1024 | tf_op jit(solution)/shard_map/pallas_call | solution.py:176
  198.4 5.4 %collective-permute-done.10.far_ref = bf16[2,1024,512]{2,1,0:T(8,128)(2,1)} collective-permute-done((bf16[2,1024,512]{2,1,0:T(8,128)(2,1)}, bf16[2,1024,512]{2,1,0:T(8,128)(2,1)}, u32[]{:S(2)}, u32[]{:S(2)}) %collective-permute-start.10) | collective-permute-done | bytes 2097184 | tf_op jit(solution)/shard_map/weights_groups1/ppermute | solution.py:511
  203.8 3.7 %shard_map.114 = bf16[2,2,1024,512]{3,2,1,0:T(8,128)(2,1)} custom-call(bf16[2,1024,512]{2,1,0:T(8,128)(2,1)} %get-tuple-element.60.near_ref, bf16[2,1024,512]{2,1,0:T(8,128)(2,1)} %collective-permute-done.10.far_ref), custom_call_target="tpu_custom_call" | custom-call | flops 1024 | bytes 1024 | tf_op jit(solution)/shard_map/pallas_call | solution.py:225
  211.0 12.4 %collective-permute-start.15 = (bf16[4,576,128]{2,1,0:T(8,128)(2,1)}, bf16[4,576,128]{2,1,0:T(8,128)(2,1)}, u32[]{:S(2)}, u32[]{:S(2)}) collective-permute-start(bf16[4,576,128]{2,1,0:T(8,128)(2,1)} %get-tuple-element.72), channel_id=1, source_target_pairs={{0,1},{1,0},{2,3},{3,2},{4,5},{5,4},{6,7},{7,6},{8,9},{9,8},{10,11... | collective-permute-start | bytes 1769480 | tf_op jit(solution)/shard_map/keys3_tensor1/ppermute | solution.py:511
  225.0 10.4 %shard_map.116 = (bf16[8,512,512]{2,1,0:T(8,128)(2,1)}, bf16[8,2048,128]{2,1,0:T(8,128)(2,1)}) custom-call(s32[1]{0:T(128)} %bitcast.9.which_ref.replica_ref, bf16[4,1024,512]{2,1,0:T(8,128)(2,1)} %get-tuple-element.63.near_ref, bf16[4,1024,512]{2,1,0:T(8,128)(2,1)} %collective-permute-done.14.far_ref), custom_call_target="tpu_custom_call" | custom-call | flops 1024 | bytes 1024 | tf_op jit(solution)/shard_map/pallas_call | solution.py:261
  237.7 5.8 %shard_map.117 = (bf16[2048,512]{1,0:T(8,128)(2,1)S(1)}, bf16[2048,64]{1,0:T(8,128)(2,1)S(1)}) custom-call(bf16[64,6144]{1,0:T(8,128)(2,1)S(1)} %copy-done.20, bf16[32,128,512]{2,1,0:T(8,128)(2,1)S(1)} %bitcast.154), custom_call_target="tpu_custom_call" | custom-call | flops 1024 | bytes 1024 | tf_op jit(solution)/shard_map/pallas_call | solution.py:336
  243.5 4.0 %shard_map.118 = (bf16[4,128,512]{2,1,0:T(8,128)(2,1)S(1)}, bf16[4,128,512]{2,1,0:T(8,128)(2,1)S(1)}) custom-call(s32[5]{0:T(128)S(1)} %pad_add_fusion.refs_0_, bf16[16,128,512]{2,1,0:T(8,128)(2,1)S(1)} %bitcast.131, bf16[16,128,512]{2,1,0:T(8,128)(2,1)S(1)} %bitcast.135, bf16[16,128,64]{2,1,0:T(8,128)(2,1)S(1)} %bitcast.140, ...), custom_call_target="tpu_custom_call" | custom-call | flops 1024 | bytes 1024 | tf_op jit(solution)/shard_map/pallas_call | solution.py:419
  247.6 5.0 %shard_map.119 = (bf16[4,128,512]{2,1,0:T(8,128)(2,1)S(1)}, bf16[4,128,512]{2,1,0:T(8,128)(2,1)S(1)}) custom-call(s32[5]{0:T(128)S(1)} %pad_add_fusion.1.refs_0_, bf16[16,128,512]{2,1,0:T(8,128)(2,1)S(1)} %bitcast.132, bf16[16,128,512]{2,1,0:T(8,128)(2,1)S(1)} %bitcast.136, bf16[16,128,64]{2,1,0:T(8,128)(2,1)S(1)} %bitcast.141, ...), custom_call_target="tpu_custom_call" | custom-call | flops 1024 | bytes 1024 | tf_op jit(solution)/shard_map/pallas_call | solution.py:419
  252.6 5.6 %shard_map.120 = (bf16[4,128,512]{2,1,0:T(8,128)(2,1)S(1)}, bf16[4,128,512]{2,1,0:T(8,128)(2,1)S(1)}) custom-call(s32[5]{0:T(128)S(1)} %pad_add_fusion.2.refs_0_, bf16[16,128,512]{2,1,0:T(8,128)(2,1)S(1)} %bitcast.133, bf16[16,128,512]{2,1,0:T(8,128)(2,1)S(1)} %bitcast.137, bf16[16,128,64]{2,1,0:T(8,128)(2,1)S(1)} %bitcast.142, ...), custom_call_target="tpu_custom_call" | custom-call | flops 1024 | bytes 1024 | tf_op jit(solution)/shard_map/pallas_call | solution.py:419
  265.0 3.3 %collective-permute-start.20 = (bf16[4,4,4096]{2,1,0:T(4,128)(2,1)S(1)}, bf16[4,4,4096]{2,1,0:T(4,128)(2,1)S(1)}, u32[]{:S(2)}, u32[]{:S(2)}) collective-permute-start(bf16[4,4,4096]{2,1,0:T(4,128)(2,1)S(1)} %bitcast.159), channel_id=1, source_target_pairs={{0,1},{1,0},{2,3},{3,2},{4,5},{5,4},{6,7},{7,6},{8,9},{9,8},{10,11... | collective-permute-start | bytes 393224 | tf_op jit(solution)/shard_map/heads_tensor1/ppermute | solution.py:511
  270.5 6.6 %collective-permute-done.16.refs_7_ = bf16[4,576,128]{2,1,0:T(8,128)(2,1)} collective-permute-done((bf16[4,576,128]{2,1,0:T(8,128)(2,1)}, bf16[4,576,128]{2,1,0:T(8,128)(2,1)}, u32[]{:S(2)}, u32[]{:S(2)}) %collective-permute-start.16) | collective-permute-done | bytes 589856 | tf_op jit(solution)/shard_map/keys3_tensor2/ppermute | solution.py:511
  277.0 5.3 %shard_map.121 = (bf16[4,128,512]{2,1,0:T(8,128)(2,1)S(1)}, bf16[4,128,512]{2,1,0:T(8,128)(2,1)S(1)}) custom-call(s32[5]{0:T(128)S(1)} %pad_add_fusion.3.refs_0_, bf16[16,128,512]{2,1,0:T(8,128)(2,1)S(1)} %bitcast.134, bf16[16,128,512]{2,1,0:T(8,128)(2,1)S(1)} %bitcast.138, bf16[16,128,64]{2,1,0:T(8,128)(2,1)S(1)} %bitcast.143, ...), custom_call_target="tpu_custom_call" | custom-call | flops 1024 | bytes 1024 | tf_op jit(solution)/shard_map/pallas_call | solution.py:419
  284.6 3.8 %collective-permute-done.21 = bf16[4,4,4096]{2,1,0:T(4,128)(2,1)S(1)} collective-permute-done((bf16[4,4,4096]{2,1,0:T(4,128)(2,1)S(1)}, bf16[4,4,4096]{2,1,0:T(4,128)(2,1)S(1)}, u32[]{:S(2)}, u32[]{:S(2)}) %collective-permute-start.21) | collective-permute-done | bytes 131104 | tf_op jit(solution)/shard_map/heads_tensor1/ppermute | solution.py:511
  288.6 12.6 %shard_map.122 = (bf16[32,3584]{1,0:T(8,128)(2,1)S(1)}, bf16[32,3584]{1,0:T(8,128)(2,1)S(1)}, bf16[32,3584]{1,0:T(8,128)(2,1)S(1)}, bf16[32,3584]{1,0:T(8,128)(2,1)S(1)}) custom-call(s32[128,1]{1,0:T(8,128)S(1)} %fusion.46.row_ref, bf16[16,4096]{1,0:T(8,128)(2,1)S(1)} %bitcast.164, bf16[16,4096]{1,0:T(8,128)(2,1)S(1)} %bitcast.163, ...), custom_call_target="tpu_custom_call" | custom-call | flops 3758096384 | bytes 29360128 | tf_op jit(solution)/shard_map/pallas_call | solution.py:464
  305.7 5.5 %collective-permute-done.22 = bf16[32,3584]{1,0:T(8,128)(2,1)S(1)} collective-permute-done((bf16[32,3584]{1,0:T(8,128)(2,1)S(1)}, bf16[32,3584]{1,0:T(8,128)(2,1)S(1)}, u32[]{:S(2)}, u32[]{:S(2)}) %collective-permute-start.22) | collective-permute-done | bytes 229408 | tf_op jit(solution)/shard_map/output_tensor1/ppermute | solution.py:511
  311.2 9.4 %collective-permute-done.23 = bf16[32,3584]{1,0:T(8,128)(2,1)S(1)} collective-permute-done((bf16[32,3584]{1,0:T(8,128)(2,1)S(1)}, bf16[32,3584]{1,0:T(8,128)(2,1)S(1)}, u32[]{:S(2)}, u32[]{:S(2)}) %collective-permute-start.23) | collective-permute-done | bytes 229408 | tf_op jit(solution)/shard_map/output_tensor2/ppermute | solution.py:511
  (190 shorter events, 74.7 us)
Async XLA Ops:
  0.0 209.9 %copy-start = (bf16[32,4,576]{2,1,0:T(4,128)(2,1)S(1)}, bf16[32,4,576]{2,1,0:T(4,128)(2,1)}, u32[]{:S(2)}) copy-start(bf16[32,4,576]{2,1,0:T(4,128)(2,1)} %param.16) | copy-start | bytes 442372
  6.8 2.3 collective-permute-start
  17.0 33.9 %all-to-all-start = ((bf16[4,4,576,128]{3,2,1,0:T(8,128)(2,1)}), bf16[4,4,576,128]{3,2,1,0:T(8,128)(2,1)}, u32[]{:S(2)}, u32[]{:S(2)}) async-start(bf16[4,4,576,128]{3,2,1,0:T(8,128)(2,1)} %shard_map.103), calls=%async_computation | async-start | bytes 4718592 | tf_op jit(solution)/shard_map/all_to_all | solution.py:597
  23.9 67.1 %collective-permute-start.5 = (bf16[1024,512]{1,0:T(8,128)(2,1)}, bf16[1024,512]{1,0:T(8,128)(2,1)}, u32[]{:S(2)}, u32[]{:S(2)}) collective-permute-start(bf16[1024,512]{1,0:T(8,128)(2,1)} %shard_map.110), channel_id=1, source_target_pairs={{0,1},{1,0},{2,3},{3,2},{4,5},{5,4},{6,7},{7,6},{8,9},{9,8},{10,11... | collective-permute-start | bytes 3145736 | tf_op jit(solution)/shard_map/weights_tensor1/ppermute | solution.py:511
  26.8 49.2 %collective-permute-start.2 = (bf16[4,576,128]{2,1,0:T(8,128)(2,1)S(1)}, bf16[4,576,128]{2,1,0:T(8,128)(2,1)S(1)}, u32[]{:S(2)}, u32[]{:S(2)}) collective-permute-start(bf16[4,576,128]{2,1,0:T(8,128)(2,1)S(1)} %bitcast.150), channel_id=1, source_target_pairs={{0,2},{1,3},{2,0},{3,1},{4,6},{5,7},{6,4},{7,5},{8,10},{9,11},{10,... | collective-permute-start | bytes 1769480 | tf_op jit(solution)/shard_map/keys0_tensor2/ppermute | solution.py:511
  29.4 46.7 %collective-permute-start.1 = (bf16[4,576,128]{2,1,0:T(8,128)(2,1)}, bf16[4,576,128]{2,1,0:T(8,128)(2,1)S(1)}, u32[]{:S(2)}, u32[]{:S(2)}) collective-permute-start(bf16[4,576,128]{2,1,0:T(8,128)(2,1)} %bitcast.3), channel_id=1, source_target_pairs={{0,1},{1,0},{2,3},{3,2},{4,5},{5,4},{6,7},{7,6},{8,9},{9,8},{10,11... | collective-permute-start | bytes 1769480 | tf_op jit(solution)/shard_map/keys0_tensor1/ppermute | solution.py:511
  29.9 61.1 %collective-permute-start.3 = (bf16[4,576,128]{2,1,0:T(8,128)(2,1)}, bf16[4,576,128]{2,1,0:T(8,128)(2,1)S(1)}, u32[]{:S(2)}, u32[]{:S(2)}) collective-permute-start(bf16[4,576,128]{2,1,0:T(8,128)(2,1)} %bitcast.3), channel_id=1, source_target_pairs={{0,3},{1,2},{2,1},{3,0},{4,7},{5,6},{6,5},{7,4},{8,11},{9,10},{10,... | collective-permute-start | bytes 1769480 | tf_op jit(solution)/shard_map/keys0_tensor3/ppermute | solution.py:511
  57.9 36.2 %copy-start.36 = (s32[128]{0:T(128)S(1)}, s32[128]{0:T(128)}, u32[]{:S(2)}) copy-start(s32[128]{0:T(128)} %param.13) | copy-start | bytes 1540
  57.9 36.5 %copy-start.31 = (bf16[32,4,2048]{2,1,0:T(4,128)(2,1)S(1)}, bf16[32,4,2048]{2,1,0:T(4,128)(2,1)}, u32[]{:S(2)}) copy-start(bf16[32,4,2048]{2,1,0:T(4,128)(2,1)} %refs_1_.1) | copy-start | bytes 1572868
  58.0 61.8 %all-to-all-start.1 = ((bf16[4,4,576,128]{3,2,1,0:T(8,128)(2,1)}), bf16[4,4,576,128]{3,2,1,0:T(8,128)(2,1)}, u32[]{:S(2)}, u32[]{:S(2)}) async-start(bf16[4,4,576,128]{3,2,1,0:T(8,128)(2,1)} %shard_map.105), calls=%async_computation.1 | async-start | bytes 4718592 | tf_op jit(solution)/shard_map/all_to_all | solution.py:597
  91.8 25.0 %collective-permute-start.6 = (bf16[1,1024,512]{2,1,0:T(8,128)(2,1)}, bf16[1,1024,512]{2,1,0:T(8,128)(2,1)}, u32[]{:S(2)}, u32[]{:S(2)}) collective-permute-start(bf16[1,1024,512]{2,1,0:T(8,128)(2,1)} %get-tuple-element.57.near_ref), channel_id=1, source_target_pairs={{0,8},{4,12},{8,0},{12,4},{1,9},{5,13},{9,1},{13,5},{2,10},{6,14},... | collective-permute-start | bytes 3145736 | tf_op jit(solution)/shard_map/weights_xfer2/ppermute | solution.py:511
  101.7 34.4 %collective-permute-start.4 = (bf16[64,6144]{1,0:T(8,128)(2,1)}, bf16[64,6144]{1,0:T(8,128)(2,1)S(1)}, u32[]{:S(2)}, u32[]{:S(2)}) collective-permute-start(bf16[64,6144]{1,0:T(8,128)(2,1)} %get-tuple-element.52), channel_id=1, source_target_pairs={{0,1},{1,0},{2,3},{3,2},{4,5},{5,4},{6,7},{7,6},{8,9},{9,8},{10,11... | collective-permute-start | bytes 2359304 | tf_op jit(solution)/shard_map/queries_tensor1/ppermute | solution.py:511
  101.7 56.6 %collective-permute-start.7 = (bf16[4,576,128]{2,1,0:T(8,128)(2,1)}, bf16[4,576,128]{2,1,0:T(8,128)(2,1)S(1)}, u32[]{:S(2)}, u32[]{:S(2)}) collective-permute-start(bf16[4,576,128]{2,1,0:T(8,128)(2,1)} %get-tuple-element.58), channel_id=1, source_target_pairs={{0,1},{1,0},{2,3},{3,2},{4,5},{5,4},{6,7},{7,6},{8,9},{9,8},{10,11... | collective-permute-start | bytes 1769480 | tf_op jit(solution)/shard_map/keys1_tensor1/ppermute | solution.py:511
  103.8 54.6 %collective-permute-start.8 = (bf16[4,576,128]{2,1,0:T(8,128)(2,1)}, bf16[4,576,128]{2,1,0:T(8,128)(2,1)S(1)}, u32[]{:S(2)}, u32[]{:S(2)}) collective-permute-start(bf16[4,576,128]{2,1,0:T(8,128)(2,1)} %get-tuple-element.59.refs_5_), channel_id=1, source_target_pairs={{0,2},{1,3},{2,0},{3,1},{4,6},{5,7},{6,4},{7,5},{8,10},{9,11},{10,... | collective-permute-start | bytes 1769480 | tf_op jit(solution)/shard_map/keys1_tensor2/ppermute | solution.py:511
  104.3 54.1 %collective-permute-start.9 = (bf16[4,576,128]{2,1,0:T(8,128)(2,1)}, bf16[4,576,128]{2,1,0:T(8,128)(2,1)}, u32[]{:S(2)}, u32[]{:S(2)}) collective-permute-start(bf16[4,576,128]{2,1,0:T(8,128)(2,1)} %get-tuple-element.58), channel_id=1, source_target_pairs={{0,3},{1,2},{2,1},{3,0},{4,7},{5,6},{6,5},{7,4},{8,11},{9,10},{10,... | collective-permute-start | bytes 1769480 | tf_op jit(solution)/shard_map/keys1_tensor3/ppermute | solution.py:511
  159.4 44.4 %collective-permute-start.10 = (bf16[2,1024,512]{2,1,0:T(8,128)(2,1)}, bf16[2,1024,512]{2,1,0:T(8,128)(2,1)}, u32[]{:S(2)}, u32[]{:S(2)}) collective-permute-start(bf16[2,1024,512]{2,1,0:T(8,128)(2,1)} %get-tuple-element.60.near_ref), channel_id=1, source_target_pairs={{0,16},{16,0},{1,17},{17,1},{2,18},{18,2},{3,19},{19,3},{4,20},{20... | collective-permute-start | bytes 6291464 | tf_op jit(solution)/shard_map/weights_groups1/ppermute | solution.py:511
  160.9 33.1 %all-to-all-start.2 = ((bf16[4,4,576,128]{3,2,1,0:T(8,128)(2,1)}), bf16[4,4,576,128]{3,2,1,0:T(8,128)(2,1)}, u32[]{:S(2)}, u32[]{:S(2)}) async-start(bf16[4,4,576,128]{3,2,1,0:T(8,128)(2,1)} %shard_map.108.refs_8_), calls=%async_computation.2 | async-start | bytes 4718592 | tf_op jit(solution)/shard_map/all_to_all | solution.py:597
  165.6 41.9 %collective-permute-start.11 = (bf16[4,576,128]{2,1,0:T(8,128)(2,1)S(1)}, bf16[4,576,128]{2,1,0:T(8,128)(2,1)S(1)}, u32[]{:S(2)}, u32[]{:S(2)}) collective-permute-start(bf16[4,576,128]{2,1,0:T(8,128)(2,1)S(1)} %copy-done.34), channel_id=1, source_target_pairs={{0,1},{1,0},{2,3},{3,2},{4,5},{5,4},{6,7},{7,6},{8,9},{9,8},{10,11... | collective-permute-start | bytes 1769480 | tf_op jit(solution)/shard_map/keys2_tensor1/ppermute | solution.py:511
  165.7 42.6 %collective-permute-start.12 = (bf16[4,576,128]{2,1,0:T(8,128)(2,1)S(1)}, bf16[4,576,128]{2,1,0:T(8,128)(2,1)}, u32[]{:S(2)}, u32[]{:S(2)}) collective-permute-start(bf16[4,576,128]{2,1,0:T(8,128)(2,1)S(1)} %copy-done.17), channel_id=1, source_target_pairs={{0,2},{1,3},{2,0},{3,1},{4,6},{5,7},{6,4},{7,5},{8,10},{9,11},{10,... | collective-permute-start | bytes 1769480 | tf_op jit(solution)/shard_map/keys2_tensor2/ppermute | solution.py:511
  167.5 40.8 %collective-permute-start.13 = (bf16[4,576,128]{2,1,0:T(8,128)(2,1)S(1)}, bf16[4,576,128]{2,1,0:T(8,128)(2,1)}, u32[]{:S(2)}, u32[]{:S(2)}) collective-permute-start(bf16[4,576,128]{2,1,0:T(8,128)(2,1)S(1)} %copy-done.34), channel_id=1, source_target_pairs={{0,3},{1,2},{2,1},{3,0},{4,7},{5,6},{6,5},{7,4},{8,11},{9,10},{10,... | collective-permute-start | bytes 1769480 | tf_op jit(solution)/shard_map/keys2_tensor3/ppermute | solution.py:511
  208.4 16.6 %collective-permute-start.14 = (bf16[4,1024,512]{2,1,0:T(8,128)(2,1)}, bf16[4,1024,512]{2,1,0:T(8,128)(2,1)}, u32[]{:S(2)}, u32[]{:S(2)}) collective-permute-start(bf16[4,1024,512]{2,1,0:T(8,128)(2,1)} %get-tuple-element.63.near_ref), channel_id=1, source_target_pairs={{0,4},{4,0},{8,12},{12,8},{1,5},{5,1},{9,13},{13,9},{2,6},{6,2},{1... | collective-permute-start | bytes 12582920 | tf_op jit(solution)/shard_map/weights_xfer1/ppermute | solution.py:511
  211.0 57.5 %collective-permute-start.15 = (bf16[4,576,128]{2,1,0:T(8,128)(2,1)}, bf16[4,576,128]{2,1,0:T(8,128)(2,1)}, u32[]{:S(2)}, u32[]{:S(2)}) collective-permute-start(bf16[4,576,128]{2,1,0:T(8,128)(2,1)} %get-tuple-element.72), channel_id=1, source_target_pairs={{0,1},{1,0},{2,3},{3,2},{4,5},{5,4},{6,7},{7,6},{8,9},{9,8},{10,11... | collective-permute-start | bytes 1769480 | tf_op jit(solution)/shard_map/keys3_tensor1/ppermute | solution.py:511
  223.4 53.6 %collective-permute-start.17 = (bf16[4,576,128]{2,1,0:T(8,128)(2,1)}, bf16[4,576,128]{2,1,0:T(8,128)(2,1)}, u32[]{:S(2)}, u32[]{:S(2)}) collective-permute-start(bf16[4,576,128]{2,1,0:T(8,128)(2,1)} %get-tuple-element.72), channel_id=1, source_target_pairs={{0,3},{1,2},{2,1},{3,0},{4,7},{5,6},{6,5},{7,4},{8,11},{9,10},{10,... | collective-permute-start | bytes 1769480 | tf_op jit(solution)/shard_map/keys3_tensor3/ppermute | solution.py:511
  224.8 52.2 %collective-permute-start.16 = (bf16[4,576,128]{2,1,0:T(8,128)(2,1)}, bf16[4,576,128]{2,1,0:T(8,128)(2,1)}, u32[]{:S(2)}, u32[]{:S(2)}) collective-permute-start(bf16[4,576,128]{2,1,0:T(8,128)(2,1)} %get-tuple-element.71.refs_5_), channel_id=1, source_target_pairs={{0,2},{1,3},{2,0},{3,1},{4,6},{5,7},{6,4},{7,5},{8,10},{9,11},{10,... | collective-permute-start | bytes 1769480 | tf_op jit(solution)/shard_map/keys3_tensor2/ppermute | solution.py:511
  265.0 23.4 %collective-permute-start.20 = (bf16[4,4,4096]{2,1,0:T(4,128)(2,1)S(1)}, bf16[4,4,4096]{2,1,0:T(4,128)(2,1)S(1)}, u32[]{:S(2)}, u32[]{:S(2)}) collective-permute-start(bf16[4,4,4096]{2,1,0:T(4,128)(2,1)S(1)} %bitcast.159), channel_id=1, source_target_pairs={{0,1},{1,0},{2,3},{3,2},{4,5},{5,4},{6,7},{7,6},{8,9},{9,8},{10,11... | collective-permute-start | bytes 393224 | tf_op jit(solution)/shard_map/heads_tensor1/ppermute | solution.py:511
  268.3 20.2 %collective-permute-start.19 = (bf16[4,4,4096]{2,1,0:T(4,128)(2,1)S(1)}, bf16[4,4,4096]{2,1,0:T(4,128)(2,1)S(1)}, u32[]{:S(2)}, u32[]{:S(2)}) collective-permute-start(bf16[4,4,4096]{2,1,0:T(4,128)(2,1)S(1)} %bitcast.157), channel_id=1, source_target_pairs={{0,1},{1,0},{2,3},{3,2},{4,5},{5,4},{6,7},{7,6},{8,9},{9,8},{10,11... | collective-permute-start | bytes 393224 | tf_op jit(solution)/shard_map/heads_tensor1/ppermute | solution.py:511
  268.4 20.1 %collective-permute-start.18 = (bf16[4,4,4096]{2,1,0:T(4,128)(2,1)S(1)}, bf16[4,4,4096]{2,1,0:T(4,128)(2,1)S(1)}, u32[]{:S(2)}, u32[]{:S(2)}) collective-permute-start(bf16[4,4,4096]{2,1,0:T(4,128)(2,1)S(1)} %bitcast.155), channel_id=1, source_target_pairs={{0,1},{1,0},{2,3},{3,2},{4,5},{5,4},{6,7},{7,6},{8,9},{9,8},{10,11... | collective-permute-start | bytes 393224 | tf_op jit(solution)/shard_map/heads_tensor1/ppermute | solution.py:511
  283.2 5.1 %collective-permute-start.21 = (bf16[4,4,4096]{2,1,0:T(4,128)(2,1)S(1)}, bf16[4,4,4096]{2,1,0:T(4,128)(2,1)S(1)}, u32[]{:S(2)}, u32[]{:S(2)}) collective-permute-start(bf16[4,4,4096]{2,1,0:T(4,128)(2,1)S(1)} %bitcast.212), channel_id=1, source_target_pairs={{0,1},{1,0},{2,3},{3,2},{4,5},{5,4},{6,7},{7,6},{8,9},{9,8},{10,11... | collective-permute-start | bytes 393224 | tf_op jit(solution)/shard_map/heads_tensor1/ppermute | solution.py:511
  288.6 32.9 %copy-start.1 = (bf16[32,4,576]{2,1,0:T(4,128)(2,1)S(1)}, bf16[32,4,576]{2,1,0:T(4,128)(2,1)}, u32[]{:S(2)}) copy-start(bf16[32,4,576]{2,1,0:T(4,128)(2,1)} %param.16) | copy-start | bytes 442372
  301.2 10.0 %collective-permute-start.22 = (bf16[32,3584]{1,0:T(8,128)(2,1)S(1)}, bf16[32,3584]{1,0:T(8,128)(2,1)S(1)}, u32[]{:S(2)}, u32[]{:S(2)}) collective-permute-start(bf16[32,3584]{1,0:T(8,128)(2,1)S(1)} %get-tuple-element.80), channel_id=1, source_target_pairs={{0,1},{1,0},{2,3},{3,2},{4,5},{5,4},{6,7},{7,6},{8,9},{9,8},{10,11... | collective-permute-start | bytes 688136 | tf_op jit(solution)/shard_map/output_tensor1/ppermute | solution.py:511
  301.6 19.1 %collective-permute-start.23 = (bf16[32,3584]{1,0:T(8,128)(2,1)S(1)}, bf16[32,3584]{1,0:T(8,128)(2,1)S(1)}, u32[]{:S(2)}, u32[]{:S(2)}) collective-permute-start(bf16[32,3584]{1,0:T(8,128)(2,1)S(1)} %get-tuple-element.81), channel_id=1, source_target_pairs={{0,2},{1,3},{2,0},{3,1},{4,6},{5,7},{6,4},{7,5},{8,10},{9,11},{10,... | collective-permute-start | bytes 688136 | tf_op jit(solution)/shard_map/output_tensor2/ppermute | solution.py:511
  303.3 17.4 %collective-permute-start.24 = (bf16[32,3584]{1,0:T(8,128)(2,1)S(1)}, bf16[32,3584]{1,0:T(8,128)(2,1)S(1)}, u32[]{:S(2)}, u32[]{:S(2)}) collective-permute-start(bf16[32,3584]{1,0:T(8,128)(2,1)S(1)} %get-tuple-element.82), channel_id=1, source_target_pairs={{0,3},{1,2},{2,1},{3,0},{4,7},{5,6},{6,5},{7,4},{8,11},{9,10},{10,... | collective-permute-start | bytes 688136 | tf_op jit(solution)/shard_map/output_tensor3/ppermute | solution.py:511
  (34 other events, 174.5 us)

commit v3 on v2

--- a/solution.py
+++ b/solution.py
@@ -630,7 +630,7 @@
     second = regroup_arrived(land(early_out), range(2, groups), me)
     sent, stack = send_keys(second, "keys1", keys[0][1:], [stack])
     keys.append(sent)
-    queries_own, queries_far = by_side([q_nope, q_rope], slots.reshape(2, half), *keys[0][1:])
+    queries_own, queries_far = by_side([q_nope, q_rope], slots.reshape(2, half), first[0])
     queries_far = across(queries_far, "tensor", 1, "queries")
     middle_out = pack_all(values, scales, request_at(middle_places), span, second[0])
     middle_in = flat(land(middle_out))

time: 324 us -> 320 us (0.988)
  local copies, waits for them, and re-layouts: 23.9 us -> 20.3 us
    unnamed x80 -> x70, local copies, waits for them, and re-layouts: 17.6 us -> 14 us
where the time goes in v3:
time: 320 us; the launch traced here: 318 us
  waiting for transfers between devices  131 us (41%)
  Pallas kernels  97.2 us (30%)
  starting transfers between devices  56.8 us (18%)
  local copies, waits for them, and re-layouts  20.3 us (6%)
  matrix products  7.04 us (2%)
  other arithmetic  5.27 us (2%)
    ppermute x25, waiting for transfers between devices, across(): lax.ppermute(x, axis, [(i, i ^ offset) for i in range(lax.axis_size(axis))])  88.1 us
    ppermute x25, starting transfers between devices, across(): lax.ppermute(x, axis, [(i, i ^ offset) for i in range(lax.axis_size(axis))])  43 us
    all_to_all x3, waiting for transfers between devices, land(): return lax.all_to_all(out, 'xfer', 0, 0, tiled=True)  42.8 us
    pallas_call x4, Pallas kernels, attend(): pl.pallas_call(lambda *refs: attend_kernel(shards, steps, score_scale, *r...  19.9 us
    pallas_call x3, Pallas kernels, pack_all(): pl.pallas_call(kernel, grid_spec=pltpu.PrefetchScalarGridSpec(num_scalar_...  14.4 us
    unnamed x70, local copies, waits for them, and re-layouts  14 us
    all_to_all x3, starting transfers between devices, land(): return lax.all_to_all(out, 'xfer', 0, 0, tiled=True)  13.8 us
    pallas_call x1, Pallas kernels, output(): pl.pallas_call(kernel, grid=(columns // width,), in_specs=[whole(row_of)]...  12.6 us
  transfers between devices with their start and end apart: 28, of which 13 were waited for; matrix products, arithmetic and copies ran while one was open for 5% of the time, Pallas kernels for 23%

profile of v3, /device:TPU:0, one launch (start us, length us, event | category | flops | bytes accessed | tf_op | source)
XLA Modules:
  0.0 318.2 jit_solution(16379233010447214513)
XLA Ops:
  2.5 4.2 %shard_map.100 = (bf16[4,576,128]{2,1,0:T(8,128)(2,1)}, bf16[4,576,128]{2,1,0:T(8,128)(2,1)}) custom-call(s32[2,4]{1,0:T(2,128)} %select_reduce_fusion.8.refs_0_, bf16[576,4096]{1,0:T(8,128)(2,1)} %bitcast.174, bf16[576,4096]{1,0:T(8,128)(2,1)} %bitcast.175, bf16[4,4096]{1,0:T(4,128)(2,1)} %bitcast.190, bf16[4,4096]{1,0:T(4,128)(2,1)} %bitcast.191), custom_call_target="tpu_custom_call" | custom-call | flops 1024 | bytes 1024 | tf_op jit(solution)/shard_map/pallas_call | solution.py:42
  12.1 4.9 %shard_map.103 = bf16[4,4,576,128]{3,2,1,0:T(8,128)(2,1)} custom-call(s32[4,4]{1,0:T(4,128)} %get-tuple-element.91.index_ref, bf16[576,4096]{1,0:T(8,128)(2,1)} %bitcast.176, bf16[576,4096]{1,0:T(8,128)(2,1)} %bitcast.177, bf16[576,4096]{1,0:T(8,128)(2,1)} %bitcast.178, bf16[576,4096]{1,0:T(8,128)(2,1)} %bitcast.179, bf16[4,4096]{1,0:T(4,128)(2,1)} %bitcast.192, ...), custom_call_target="tpu_custom_call" | custom-call | flops 1024 | bytes 1024 | tf_op jit(solution)/shard_map/pallas_call | solution.py:70
  17.0 4.5 %all-to-all-start = ((bf16[4,4,576,128]{3,2,1,0:T(8,128)(2,1)}), bf16[4,4,576,128]{3,2,1,0:T(8,128)(2,1)}, u32[]{:S(2)}, u32[]{:S(2)}) async-start(bf16[4,4,576,128]{3,2,1,0:T(8,128)(2,1)} %shard_map.103), calls=%async_computation | async-start | bytes 4718592 | tf_op jit(solution)/shard_map/all_to_all | solution.py:597
  31.2 19.6 %all-to-all-done.refs_0_.refs_1_.refs_2_.refs_3_ = bf16[4,4,576,128]{3,2,1,0:T(8,128)(2,1)} async-done(((bf16[4,4,576,128]{3,2,1,0:T(8,128)(2,1)}), bf16[4,4,576,128]{3,2,1,0:T(8,128)(2,1)}, u32[]{:S(2)}, u32[]{:S(2)}) %all-to-all-start) | async-done | bytes 2359328 | tf_op jit(solution)/shard_map/all_to_all | solution.py:597
  53.1 4.8 %shard_map.105 = bf16[4,4,576,128]{3,2,1,0:T(8,128)(2,1)} custom-call(s32[4,4]{1,0:T(4,128)} %get-tuple-element.92.index_ref, bf16[576,4096]{1,0:T(8,128)(2,1)} %bitcast.180, bf16[576,4096]{1,0:T(8,128)(2,1)} %bitcast.181, bf16[576,4096]{1,0:T(8,128)(2,1)} %bitcast.182, bf16[576,4096]{1,0:T(8,128)(2,1)} %bitcast.183, bf16[4,4096]{1,0:T(4,128)(2,1)} %bitcast.196, ...), custom_call_target="tpu_custom_call" | custom-call | flops 1024 | bytes 1024 | tf_op jit(solution)/shard_map/pallas_call | solution.py:70
  58.0 4.6 %all-to-all-start.1 = ((bf16[4,4,576,128]{3,2,1,0:T(8,128)(2,1)}), bf16[4,4,576,128]{3,2,1,0:T(8,128)(2,1)}, u32[]{:S(2)}, u32[]{:S(2)}) async-start(bf16[4,4,576,128]{3,2,1,0:T(8,128)(2,1)} %shard_map.105), calls=%async_computation.1 | async-start | bytes 4718592 | tf_op jit(solution)/shard_map/all_to_all | solution.py:597
  63.6 12.5 %collective-permute-done.2.refs_8_.refs_3_.refs_6_ = bf16[4,576,128]{2,1,0:T(8,128)(2,1)S(1)} collective-permute-done((bf16[4,576,128]{2,1,0:T(8,128)(2,1)S(1)}, bf16[4,576,128]{2,1,0:T(8,128)(2,1)S(1)}, u32[]{:S(2)}, u32[]{:S(2)}) %collective-permute-start.2) | collective-permute-done | bytes 589856 | tf_op jit(solution)/shard_map/keys0_tensor1/ppermute | solution.py:511
  76.1 14.9 %collective-permute-done.4.refs_10_.refs_5_.refs_8_ = bf16[4,576,128]{2,1,0:T(8,128)(2,1)S(1)} collective-permute-done((bf16[4,576,128]{2,1,0:T(8,128)(2,1)S(1)}, bf16[4,576,128]{2,1,0:T(8,128)(2,1)S(1)}, u32[]{:S(2)}, u32[]{:S(2)}) %collective-permute-start.4) | collective-permute-done | bytes 589856 | tf_op jit(solution)/shard_map/keys0_tensor3/ppermute | solution.py:511
  103.8 4.7 %shard_map.108.refs_8_ = bf16[4,4,576,128]{3,2,1,0:T(8,128)(2,1)} custom-call(s32[4,4]{1,0:T(4,128)} %get-tuple-element.90.index_ref, bf16[576,4096]{1,0:T(8,128)(2,1)} %bitcast.184, bf16[576,4096]{1,0:T(8,128)(2,1)} %bitcast.185, bf16[576,4096]{1,0:T(8,128)(2,1)} %bitcast.186, bf16[576,4096]{1,0:T(8,128)(2,1)} %bitcast.187, bf16[4,4096]{1,0:T(4,128)(2,1)} %bitcast.200, ...), custom_call_target="tpu_custom_call" | custom-call | flops 1024 | bytes 1024 | tf_op jit(solution)/shard_map/pallas_call | solution.py:70
  108.5 8.3 %collective-permute-done.6.far_ref = bf16[1,1024,512]{2,1,0:T(8,128)(2,1)} collective-permute-done((bf16[1,1024,512]{2,1,0:T(8,128)(2,1)}, bf16[1,1024,512]{2,1,0:T(8,128)(2,1)}, u32[]{:S(2)}, u32[]{:S(2)}) %collective-permute-start.6) | collective-permute-done | bytes 1048608 | tf_op jit(solution)/shard_map/weights_xfer2/ppermute | solution.py:511
  116.9 3.0 shard_map.112
  120.4 4.2 %shard_map.106 = (bf16[4,576,128]{2,1,0:T(8,128)(2,1)}, bf16[4,576,128]{2,1,0:T(8,128)(2,1)}) custom-call(s32[2,4]{1,0:T(2,128)} %broadcast_10_refs_0_.2.refs_0_, s32[2,4]{1,0:T(2,128)} %get-tuple-element.97.refs_1_, bf16[16,576,128]{2,1,0:T(8,128)(2,1)} %bitcast.6.refs_2_.refs_3_.refs_4_, bf16[16,576,128]{2,1,0:T(8,128)(2,1)} %bitcast.6.refs_2_.refs_3_.refs_4_), custom_call_target="tpu_custom_call" | custom-call | flops 1024 | bytes 1024 | tf_op jit(solution)/shard_map/pallas_call | solution.py:176
  127.9 5.8 %shard_map.107 = (bf16[2048,512]{1,0:T(8,128)(2,1)S(1)}, bf16[2048,64]{1,0:T(8,128)(2,1)S(1)}) custom-call(bf16[64,6144]{1,0:T(8,128)(2,1)S(1)} %get-tuple-element.47.queries_ref, bf16[32,128,512]{2,1,0:T(8,128)(2,1)S(1)} %copy-done.4, bf16[4,576,128]{2,1,0:T(8,128)(2,1)S(1)} %copy-done.13), custom_call_target="tpu_custom_call" | custom-call | flops 1024 | bytes 1024 | tf_op jit(solution)/shard_map/pallas_call | solution.py:336
  135.0 20.3 %collective-permute-done.7.refs_3_.refs_6_ = bf16[4,576,128]{2,1,0:T(8,128)(2,1)S(1)} collective-permute-done((bf16[4,576,128]{2,1,0:T(8,128)(2,1)}, bf16[4,576,128]{2,1,0:T(8,128)(2,1)S(1)}, u32[]{:S(2)}, u32[]{:S(2)}) %collective-permute-start.7) | collective-permute-done | bytes 589856 | tf_op jit(solution)/shard_map/keys1_tensor1/ppermute | solution.py:511
  157.6 4.7 %all-to-all-start.2 = ((bf16[4,4,576,128]{3,2,1,0:T(8,128)(2,1)}), bf16[4,4,576,128]{3,2,1,0:T(8,128)(2,1)}, u32[]{:S(2)}, u32[]{:S(2)}) async-start(bf16[4,4,576,128]{3,2,1,0:T(8,128)(2,1)} %shard_map.108.refs_8_), calls=%async_computation.2 | async-start | bytes 4718592 | tf_op jit(solution)/shard_map/all_to_all | solution.py:597
  167.5 23.2 %all-to-all-done.2 = bf16[4,4,576,128]{3,2,1,0:T(8,128)(2,1)} async-done(((bf16[4,4,576,128]{3,2,1,0:T(8,128)(2,1)}), bf16[4,4,576,128]{3,2,1,0:T(8,128)(2,1)}, u32[]{:S(2)}, u32[]{:S(2)}) %all-to-all-start.2) | async-done | bytes 2359328 | tf_op jit(solution)/shard_map/all_to_all | solution.py:597
  190.7 4.4 %shard_map.109 = (bf16[4,576,128]{2,1,0:T(8,128)(2,1)}, bf16[4,576,128]{2,1,0:T(8,128)(2,1)}) custom-call(s32[2,4]{1,0:T(2,128)} %slice.35.refs_0_, s32[2,4]{1,0:T(2,128)} %get-tuple-element.96.refs_1_, bf16[16,576,128]{2,1,0:T(8,128)(2,1)} %bitcast.6.refs_2_.refs_3_.refs_4_, bf16[16,576,128]{2,1,0:T(8,128)(2,1)} %bitcast.10.refs_3_.refs_5_, ...), custom_call_target="tpu_custom_call" | custom-call | flops 1024 | bytes 1024 | tf_op jit(solution)/shard_map/pallas_call | solution.py:176
  195.1 5.7 %collective-permute-done.10.far_ref = bf16[2,1024,512]{2,1,0:T(8,128)(2,1)} collective-permute-done((bf16[2,1024,512]{2,1,0:T(8,128)(2,1)}, bf16[2,1024,512]{2,1,0:T(8,128)(2,1)}, u32[]{:S(2)}, u32[]{:S(2)}) %collective-permute-start.10) | collective-permute-done | bytes 2097184 | tf_op jit(solution)/shard_map/weights_groups1/ppermute | solution.py:511
  200.8 3.7 %shard_map.114 = bf16[2,2,1024,512]{3,2,1,0:T(8,128)(2,1)} custom-call(bf16[2,1024,512]{2,1,0:T(8,128)(2,1)} %get-tuple-element.60.near_ref, bf16[2,1024,512]{2,1,0:T(8,128)(2,1)} %collective-permute-done.10.far_ref), custom_call_target="tpu_custom_call" | custom-call | flops 1024 | bytes 1024 | tf_op jit(solution)/shard_map/pallas_call | solution.py:225
  208.3 11.7 %collective-permute-start.15 = (bf16[4,576,128]{2,1,0:T(8,128)(2,1)}, bf16[4,576,128]{2,1,0:T(8,128)(2,1)}, u32[]{:S(2)}, u32[]{:S(2)}) collective-permute-start(bf16[4,576,128]{2,1,0:T(8,128)(2,1)} %get-tuple-element.72), channel_id=1, source_target_pairs={{0,1},{1,0},{2,3},{3,2},{4,5},{5,4},{6,7},{7,6},{8,9},{9,8},{10,11... | collective-permute-start | bytes 1769480 | tf_op jit(solution)/shard_map/keys3_tensor1/ppermute | solution.py:511
  221.6 10.3 %shard_map.116 = (bf16[8,512,512]{2,1,0:T(8,128)(2,1)}, bf16[8,2048,128]{2,1,0:T(8,128)(2,1)}) custom-call(s32[1]{0:T(128)} %bitcast.8.which_ref.replica_ref, bf16[4,1024,512]{2,1,0:T(8,128)(2,1)} %get-tuple-element.63.near_ref, bf16[4,1024,512]{2,1,0:T(8,128)(2,1)} %collective-permute-done.14.far_ref), custom_call_target="tpu_custom_call" | custom-call | flops 1024 | bytes 1024 | tf_op jit(solution)/shard_map/pallas_call | solution.py:261
  234.3 5.8 %shard_map.117 = (bf16[2048,512]{1,0:T(8,128)(2,1)S(1)}, bf16[2048,64]{1,0:T(8,128)(2,1)S(1)}) custom-call(bf16[64,6144]{1,0:T(8,128)(2,1)S(1)} %copy-done.17, bf16[32,128,512]{2,1,0:T(8,128)(2,1)S(1)} %bitcast.155), custom_call_target="tpu_custom_call" | custom-call | flops 1024 | bytes 1024 | tf_op jit(solution)/shard_map/pallas_call | solution.py:336
  240.1 4.0 %shard_map.118 = (bf16[4,128,512]{2,1,0:T(8,128)(2,1)S(1)}, bf16[4,128,512]{2,1,0:T(8,128)(2,1)S(1)}) custom-call(s32[5]{0:T(128)S(1)} %pad_add_fusion.refs_0_, bf16[16,128,512]{2,1,0:T(8,128)(2,1)S(1)} %bitcast.131, bf16[16,128,512]{2,1,0:T(8,128)(2,1)S(1)} %bitcast.135, bf16[16,128,64]{2,1,0:T(8,128)(2,1)S(1)} %bitcast.145, ...), custom_call_target="tpu_custom_call" | custom-call | flops 1024 | bytes 1024 | tf_op jit(solution)/shard_map/pallas_call | solution.py:419
  244.2 5.1 %shard_map.119 = (bf16[4,128,512]{2,1,0:T(8,128)(2,1)S(1)}, bf16[4,128,512]{2,1,0:T(8,128)(2,1)S(1)}) custom-call(s32[5]{0:T(128)S(1)} %pad_add_fusion.1.refs_0_, bf16[16,128,512]{2,1,0:T(8,128)(2,1)S(1)} %bitcast.132, bf16[16,128,512]{2,1,0:T(8,128)(2,1)S(1)} %bitcast.136, bf16[16,128,64]{2,1,0:T(8,128)(2,1)S(1)} %bitcast.146, ...), custom_call_target="tpu_custom_call" | custom-call | flops 1024 | bytes 1024 | tf_op jit(solution)/shard_map/pallas_call | solution.py:419
  249.4 5.5 %shard_map.120 = (bf16[4,128,512]{2,1,0:T(8,128)(2,1)S(1)}, bf16[4,128,512]{2,1,0:T(8,128)(2,1)S(1)}) custom-call(s32[5]{0:T(128)S(1)} %pad_add_fusion.2.refs_0_, bf16[16,128,512]{2,1,0:T(8,128)(2,1)S(1)} %bitcast.133, bf16[16,128,512]{2,1,0:T(8,128)(2,1)S(1)} %bitcast.137, bf16[16,128,64]{2,1,0:T(8,128)(2,1)S(1)} %bitcast.147, ...), custom_call_target="tpu_custom_call" | custom-call | flops 1024 | bytes 1024 | tf_op jit(solution)/shard_map/pallas_call | solution.py:419
  261.6 3.3 %collective-permute-start.20 = (bf16[4,4,4096]{2,1,0:T(4,128)(2,1)S(1)}, bf16[4,4,4096]{2,1,0:T(4,128)(2,1)S(1)}, u32[]{:S(2)}, u32[]{:S(2)}) collective-permute-start(bf16[4,4,4096]{2,1,0:T(4,128)(2,1)S(1)} %bitcast.160), channel_id=1, source_target_pairs={{0,1},{1,0},{2,3},{3,2},{4,5},{5,4},{6,7},{7,6},{8,9},{9,8},{10,11... | collective-permute-start | bytes 393224 | tf_op jit(solution)/shard_map/heads_tensor1/ppermute | solution.py:511
  267.1 6.6 %collective-permute-done.16.refs_7_ = bf16[4,576,128]{2,1,0:T(8,128)(2,1)} collective-permute-done((bf16[4,576,128]{2,1,0:T(8,128)(2,1)}, bf16[4,576,128]{2,1,0:T(8,128)(2,1)}, u32[]{:S(2)}, u32[]{:S(2)}) %collective-permute-start.16) | collective-permute-done | bytes 589856 | tf_op jit(solution)/shard_map/keys3_tensor2/ppermute | solution.py:511
  273.6 5.3 %shard_map.121 = (bf16[4,128,512]{2,1,0:T(8,128)(2,1)S(1)}, bf16[4,128,512]{2,1,0:T(8,128)(2,1)S(1)}) custom-call(s32[5]{0:T(128)S(1)} %pad_add_fusion.3.refs_0_, bf16[16,128,512]{2,1,0:T(8,128)(2,1)S(1)} %bitcast.134, bf16[16,128,512]{2,1,0:T(8,128)(2,1)S(1)} %bitcast.138, bf16[16,128,64]{2,1,0:T(8,128)(2,1)S(1)} %bitcast.148, ...), custom_call_target="tpu_custom_call" | custom-call | flops 1024 | bytes 1024 | tf_op jit(solution)/shard_map/pallas_call | solution.py:419
  281.3 3.8 %collective-permute-done.21 = bf16[4,4,4096]{2,1,0:T(4,128)(2,1)S(1)} collective-permute-done((bf16[4,4,4096]{2,1,0:T(4,128)(2,1)S(1)}, bf16[4,4,4096]{2,1,0:T(4,128)(2,1)S(1)}, u32[]{:S(2)}, u32[]{:S(2)}) %collective-permute-start.21) | collective-permute-done | bytes 131104 | tf_op jit(solution)/shard_map/heads_tensor1/ppermute | solution.py:511
  285.2 12.6 %shard_map.122 = (bf16[32,3584]{1,0:T(8,128)(2,1)S(1)}, bf16[32,3584]{1,0:T(8,128)(2,1)S(1)}, bf16[32,3584]{1,0:T(8,128)(2,1)S(1)}, bf16[32,3584]{1,0:T(8,128)(2,1)S(1)}) custom-call(s32[128,1]{1,0:T(8,128)S(1)} %fusion.46.row_ref, bf16[16,4096]{1,0:T(8,128)(2,1)S(1)} %bitcast.165, bf16[16,4096]{1,0:T(8,128)(2,1)S(1)} %bitcast.164, ...), custom_call_target="tpu_custom_call" | custom-call | flops 3758096384 | bytes 29360128 | tf_op jit(solution)/shard_map/pallas_call | solution.py:464
  302.3 5.5 %collective-permute-done.22 = bf16[32,3584]{1,0:T(8,128)(2,1)S(1)} collective-permute-done((bf16[32,3584]{1,0:T(8,128)(2,1)S(1)}, bf16[32,3584]{1,0:T(8,128)(2,1)S(1)}, u32[]{:S(2)}, u32[]{:S(2)}) %collective-permute-start.22) | collective-permute-done | bytes 229408 | tf_op jit(solution)/shard_map/output_tensor1/ppermute | solution.py:511
  307.8 9.5 %collective-permute-done.23 = bf16[32,3584]{1,0:T(8,128)(2,1)S(1)} collective-permute-done((bf16[32,3584]{1,0:T(8,128)(2,1)S(1)}, bf16[32,3584]{1,0:T(8,128)(2,1)S(1)}, u32[]{:S(2)}, u32[]{:S(2)}) %collective-permute-start.23) | collective-permute-done | bytes 229408 | tf_op jit(solution)/shard_map/output_tensor2/ppermute | solution.py:511
  (180 shorter events, 70.6 us)
Async XLA Ops:
  0.0 207.3 %copy-start = (bf16[32,4,576]{2,1,0:T(4,128)(2,1)S(1)}, bf16[32,4,576]{2,1,0:T(4,128)(2,1)}, u32[]{:S(2)}) copy-start(bf16[32,4,576]{2,1,0:T(4,128)(2,1)} %param.16) | copy-start | bytes 442372
  6.7 2.3 collective-permute-start
  17.0 33.9 %all-to-all-start = ((bf16[4,4,576,128]{3,2,1,0:T(8,128)(2,1)}), bf16[4,4,576,128]{3,2,1,0:T(8,128)(2,1)}, u32[]{:S(2)}, u32[]{:S(2)}) async-start(bf16[4,4,576,128]{3,2,1,0:T(8,128)(2,1)} %shard_map.103), calls=%async_computation | async-start | bytes 4718592 | tf_op jit(solution)/shard_map/all_to_all | solution.py:597
  23.9 67.1 %collective-permute-start.5 = (bf16[1024,512]{1,0:T(8,128)(2,1)}, bf16[1024,512]{1,0:T(8,128)(2,1)}, u32[]{:S(2)}, u32[]{:S(2)}) collective-permute-start(bf16[1024,512]{1,0:T(8,128)(2,1)} %shard_map.110), channel_id=1, source_target_pairs={{0,1},{1,0},{2,3},{3,2},{4,5},{5,4},{6,7},{7,6},{8,9},{9,8},{10,11... | collective-permute-start | bytes 3145736 | tf_op jit(solution)/shard_map/weights_tensor1/ppermute | solution.py:511
  26.9 49.2 %collective-permute-start.3 = (bf16[4,576,128]{2,1,0:T(8,128)(2,1)S(1)}, bf16[4,576,128]{2,1,0:T(8,128)(2,1)S(1)}, u32[]{:S(2)}, u32[]{:S(2)}) collective-permute-start(bf16[4,576,128]{2,1,0:T(8,128)(2,1)S(1)} %bitcast.142), channel_id=1, source_target_pairs={{0,2},{1,3},{2,0},{3,1},{4,6},{5,7},{6,4},{7,5},{8,10},{9,11},{10,... | collective-permute-start | bytes 1769480 | tf_op jit(solution)/shard_map/keys0_tensor2/ppermute | solution.py:511
  29.5 46.6 %collective-permute-start.2 = (bf16[4,576,128]{2,1,0:T(8,128)(2,1)S(1)}, bf16[4,576,128]{2,1,0:T(8,128)(2,1)S(1)}, u32[]{:S(2)}, u32[]{:S(2)}) collective-permute-start(bf16[4,576,128]{2,1,0:T(8,128)(2,1)S(1)} %bitcast.219), channel_id=1, source_target_pairs={{0,1},{1,0},{2,3},{3,2},{4,5},{5,4},{6,7},{7,6},{8,9},{9,8},{10,11... | collective-permute-start | bytes 1769480 | tf_op jit(solution)/shard_map/keys0_tensor1/ppermute | solution.py:511
  29.9 61.1 %collective-permute-start.4 = (bf16[4,576,128]{2,1,0:T(8,128)(2,1)S(1)}, bf16[4,576,128]{2,1,0:T(8,128)(2,1)S(1)}, u32[]{:S(2)}, u32[]{:S(2)}) collective-permute-start(bf16[4,576,128]{2,1,0:T(8,128)(2,1)S(1)} %bitcast.220), channel_id=1, source_target_pairs={{0,3},{1,2},{2,1},{3,0},{4,7},{5,6},{6,5},{7,4},{8,11},{9,10},{10,... | collective-permute-start | bytes 1769480 | tf_op jit(solution)/shard_map/keys0_tensor3/ppermute | solution.py:511
  57.9 36.2 %copy-start.30 = (s32[128]{0:T(128)S(1)}, s32[128]{0:T(128)}, u32[]{:S(2)}) copy-start(s32[128]{0:T(128)} %param.13) | copy-start | bytes 1540
  58.0 61.9 %all-to-all-start.1 = ((bf16[4,4,576,128]{3,2,1,0:T(8,128)(2,1)}), bf16[4,4,576,128]{3,2,1,0:T(8,128)(2,1)}, u32[]{:S(2)}, u32[]{:S(2)}) async-start(bf16[4,4,576,128]{3,2,1,0:T(8,128)(2,1)} %shard_map.105), calls=%async_computation.1 | async-start | bytes 4718592 | tf_op jit(solution)/shard_map/all_to_all | solution.py:597
  91.8 25.0 %collective-permute-start.6 = (bf16[1,1024,512]{2,1,0:T(8,128)(2,1)}, bf16[1,1024,512]{2,1,0:T(8,128)(2,1)}, u32[]{:S(2)}, u32[]{:S(2)}) collective-permute-start(bf16[1,1024,512]{2,1,0:T(8,128)(2,1)} %get-tuple-element.57.near_ref), channel_id=1, source_target_pairs={{0,8},{4,12},{8,0},{12,4},{1,9},{5,13},{9,1},{13,5},{2,10},{6,14},... | collective-permute-start | bytes 3145736 | tf_op jit(solution)/shard_map/weights_xfer2/ppermute | solution.py:511
  98.7 36.3 %collective-permute-start.1 = (bf16[64,6144]{1,0:T(8,128)(2,1)}, bf16[64,6144]{1,0:T(8,128)(2,1)S(1)}, u32[]{:S(2)}, u32[]{:S(2)}) collective-permute-start(bf16[64,6144]{1,0:T(8,128)(2,1)} %get-tuple-element.51), channel_id=1, source_target_pairs={{0,1},{1,0},{2,3},{3,2},{4,5},{5,4},{6,7},{7,6},{8,9},{9,8},{10,11... | collective-permute-start | bytes 2359304 | tf_op jit(solution)/shard_map/queries_tensor1/ppermute | solution.py:511
  98.7 56.6 %collective-permute-start.7 = (bf16[4,576,128]{2,1,0:T(8,128)(2,1)}, bf16[4,576,128]{2,1,0:T(8,128)(2,1)S(1)}, u32[]{:S(2)}, u32[]{:S(2)}) collective-permute-start(bf16[4,576,128]{2,1,0:T(8,128)(2,1)} %get-tuple-element.58), channel_id=1, source_target_pairs={{0,1},{1,0},{2,3},{3,2},{4,5},{5,4},{6,7},{7,6},{8,9},{9,8},{10,11... | collective-permute-start | bytes 1769480 | tf_op jit(solution)/shard_map/keys1_tensor1/ppermute | solution.py:511
  100.7 54.6 %collective-permute-start.8 = (bf16[4,576,128]{2,1,0:T(8,128)(2,1)}, bf16[4,576,128]{2,1,0:T(8,128)(2,1)}, u32[]{:S(2)}, u32[]{:S(2)}) collective-permute-start(bf16[4,576,128]{2,1,0:T(8,128)(2,1)} %get-tuple-element.59.refs_5_), channel_id=1, source_target_pairs={{0,2},{1,3},{2,0},{3,1},{4,6},{5,7},{6,4},{7,5},{8,10},{9,11},{10,... | collective-permute-start | bytes 1769480 | tf_op jit(solution)/shard_map/keys1_tensor2/ppermute | solution.py:511
  101.2 54.1 %collective-permute-start.9 = (bf16[4,576,128]{2,1,0:T(8,128)(2,1)}, bf16[4,576,128]{2,1,0:T(8,128)(2,1)}, u32[]{:S(2)}, u32[]{:S(2)}) collective-permute-start(bf16[4,576,128]{2,1,0:T(8,128)(2,1)} %get-tuple-element.58), channel_id=1, source_target_pairs={{0,3},{1,2},{2,1},{3,0},{4,7},{5,6},{6,5},{7,4},{8,11},{9,10},{10,... | collective-permute-start | bytes 1769480 | tf_op jit(solution)/shard_map/keys1_tensor3/ppermute | solution.py:511
  135.0 20.3 %copy-start.16 = (bf16[64,6144]{1,0:T(8,128)(2,1)}, bf16[64,6144]{1,0:T(8,128)(2,1)S(1)}, u32[]{:S(2)}) copy-start(bf16[64,6144]{1,0:T(8,128)(2,1)S(1)} %collective-permute-done.1.refs_6_.queries_ref) | copy-start | bytes 2359300
  156.1 44.6 %collective-permute-start.10 = (bf16[2,1024,512]{2,1,0:T(8,128)(2,1)}, bf16[2,1024,512]{2,1,0:T(8,128)(2,1)}, u32[]{:S(2)}, u32[]{:S(2)}) collective-permute-start(bf16[2,1024,512]{2,1,0:T(8,128)(2,1)} %get-tuple-element.60.near_ref), channel_id=1, source_target_pairs={{0,16},{16,0},{1,17},{17,1},{2,18},{18,2},{3,19},{19,3},{4,20},{20... | collective-permute-start | bytes 6291464 | tf_op jit(solution)/shard_map/weights_groups1/ppermute | solution.py:511
  157.6 33.1 %all-to-all-start.2 = ((bf16[4,4,576,128]{3,2,1,0:T(8,128)(2,1)}), bf16[4,4,576,128]{3,2,1,0:T(8,128)(2,1)}, u32[]{:S(2)}, u32[]{:S(2)}) async-start(bf16[4,4,576,128]{3,2,1,0:T(8,128)(2,1)} %shard_map.108.refs_8_), calls=%async_computation.2 | async-start | bytes 4718592 | tf_op jit(solution)/shard_map/all_to_all | solution.py:597
  162.3 42.1 %collective-permute-start.11 = (bf16[4,576,128]{2,1,0:T(8,128)(2,1)}, bf16[4,576,128]{2,1,0:T(8,128)(2,1)S(1)}, u32[]{:S(2)}, u32[]{:S(2)}) collective-permute-start(bf16[4,576,128]{2,1,0:T(8,128)(2,1)} %get-tuple-element.61), channel_id=1, source_target_pairs={{0,1},{1,0},{2,3},{3,2},{4,5},{5,4},{6,7},{7,6},{8,9},{9,8},{10,11... | collective-permute-start | bytes 1769480 | tf_op jit(solution)/shard_map/keys2_tensor1/ppermute | solution.py:511
  162.4 42.5 %collective-permute-start.12 = (bf16[4,576,128]{2,1,0:T(8,128)(2,1)S(1)}, bf16[4,576,128]{2,1,0:T(8,128)(2,1)S(1)}, u32[]{:S(2)}, u32[]{:S(2)}) collective-permute-start(bf16[4,576,128]{2,1,0:T(8,128)(2,1)S(1)} %copy-done.14), channel_id=1, source_target_pairs={{0,2},{1,3},{2,0},{3,1},{4,6},{5,7},{6,4},{7,5},{8,10},{9,11},{10,... | collective-permute-start | bytes 1769480 | tf_op jit(solution)/shard_map/keys2_tensor2/ppermute | solution.py:511
  164.4 40.5 %collective-permute-start.13 = (bf16[4,576,128]{2,1,0:T(8,128)(2,1)}, bf16[4,576,128]{2,1,0:T(8,128)(2,1)}, u32[]{:S(2)}, u32[]{:S(2)}) collective-permute-start(bf16[4,576,128]{2,1,0:T(8,128)(2,1)} %get-tuple-element.61), channel_id=1, source_target_pairs={{0,3},{1,2},{2,1},{3,0},{4,7},{5,6},{6,5},{7,4},{8,11},{9,10},{10,... | collective-permute-start | bytes 1769480 | tf_op jit(solution)/shard_map/keys2_tensor3/ppermute | solution.py:511
  205.7 15.9 %collective-permute-start.14 = (bf16[4,1024,512]{2,1,0:T(8,128)(2,1)}, bf16[4,1024,512]{2,1,0:T(8,128)(2,1)}, u32[]{:S(2)}, u32[]{:S(2)}) collective-permute-start(bf16[4,1024,512]{2,1,0:T(8,128)(2,1)} %get-tuple-element.63.near_ref), channel_id=1, source_target_pairs={{0,4},{4,0},{8,12},{12,8},{1,5},{5,1},{9,13},{13,9},{2,6},{6,2},{1... | collective-permute-start | bytes 12582920 | tf_op jit(solution)/shard_map/weights_xfer1/ppermute | solution.py:511
  208.3 56.7 %collective-permute-start.15 = (bf16[4,576,128]{2,1,0:T(8,128)(2,1)}, bf16[4,576,128]{2,1,0:T(8,128)(2,1)}, u32[]{:S(2)}, u32[]{:S(2)}) collective-permute-start(bf16[4,576,128]{2,1,0:T(8,128)(2,1)} %get-tuple-element.72), channel_id=1, source_target_pairs={{0,1},{1,0},{2,3},{3,2},{4,5},{5,4},{6,7},{7,6},{8,9},{9,8},{10,11... | collective-permute-start | bytes 1769480 | tf_op jit(solution)/shard_map/keys3_tensor1/ppermute | solution.py:511
  220.1 53.6 %collective-permute-start.17 = (bf16[4,576,128]{2,1,0:T(8,128)(2,1)}, bf16[4,576,128]{2,1,0:T(8,128)(2,1)}, u32[]{:S(2)}, u32[]{:S(2)}) collective-permute-start(bf16[4,576,128]{2,1,0:T(8,128)(2,1)} %get-tuple-element.72), channel_id=1, source_target_pairs={{0,3},{1,2},{2,1},{3,0},{4,7},{5,6},{6,5},{7,4},{8,11},{9,10},{10,... | collective-permute-start | bytes 1769480 | tf_op jit(solution)/shard_map/keys3_tensor3/ppermute | solution.py:511
  221.5 52.1 %collective-permute-start.16 = (bf16[4,576,128]{2,1,0:T(8,128)(2,1)}, bf16[4,576,128]{2,1,0:T(8,128)(2,1)}, u32[]{:S(2)}, u32[]{:S(2)}) collective-permute-start(bf16[4,576,128]{2,1,0:T(8,128)(2,1)} %get-tuple-element.71.refs_5_), channel_id=1, source_target_pairs={{0,2},{1,3},{2,0},{3,1},{4,6},{5,7},{6,4},{7,5},{8,10},{9,11},{10,... | collective-permute-start | bytes 1769480 | tf_op jit(solution)/shard_map/keys3_tensor2/ppermute | solution.py:511
  261.6 23.4 %collective-permute-start.20 = (bf16[4,4,4096]{2,1,0:T(4,128)(2,1)S(1)}, bf16[4,4,4096]{2,1,0:T(4,128)(2,1)S(1)}, u32[]{:S(2)}, u32[]{:S(2)}) collective-permute-start(bf16[4,4,4096]{2,1,0:T(4,128)(2,1)S(1)} %bitcast.160), channel_id=1, source_target_pairs={{0,1},{1,0},{2,3},{3,2},{4,5},{5,4},{6,7},{7,6},{8,9},{9,8},{10,11... | collective-permute-start | bytes 393224 | tf_op jit(solution)/shard_map/heads_tensor1/ppermute | solution.py:511
  264.9 20.2 %collective-permute-start.19 = (bf16[4,4,4096]{2,1,0:T(4,128)(2,1)S(1)}, bf16[4,4,4096]{2,1,0:T(4,128)(2,1)S(1)}, u32[]{:S(2)}, u32[]{:S(2)}) collective-permute-start(bf16[4,4,4096]{2,1,0:T(4,128)(2,1)S(1)} %bitcast.158), channel_id=1, source_target_pairs={{0,1},{1,0},{2,3},{3,2},{4,5},{5,4},{6,7},{7,6},{8,9},{9,8},{10,11... | collective-permute-start | bytes 393224 | tf_op jit(solution)/shard_map/heads_tensor1/ppermute | solution.py:511
  265.0 20.1 %collective-permute-start.18 = (bf16[4,4,4096]{2,1,0:T(4,128)(2,1)S(1)}, bf16[4,4,4096]{2,1,0:T(4,128)(2,1)S(1)}, u32[]{:S(2)}, u32[]{:S(2)}) collective-permute-start(bf16[4,4,4096]{2,1,0:T(4,128)(2,1)S(1)} %bitcast.156), channel_id=1, source_target_pairs={{0,1},{1,0},{2,3},{3,2},{4,5},{5,4},{6,7},{7,6},{8,9},{9,8},{10,11... | collective-permute-start | bytes 393224 | tf_op jit(solution)/shard_map/heads_tensor1/ppermute | solution.py:511
  279.9 5.1 %collective-permute-start.21 = (bf16[4,4,4096]{2,1,0:T(4,128)(2,1)S(1)}, bf16[4,4,4096]{2,1,0:T(4,128)(2,1)S(1)}, u32[]{:S(2)}, u32[]{:S(2)}) collective-permute-start(bf16[4,4,4096]{2,1,0:T(4,128)(2,1)S(1)} %bitcast.213), channel_id=1, source_target_pairs={{0,1},{1,0},{2,3},{3,2},{4,5},{5,4},{6,7},{7,6},{8,9},{9,8},{10,11... | collective-permute-start | bytes 393224 | tf_op jit(solution)/shard_map/heads_tensor1/ppermute | solution.py:511
  285.2 33.0 %copy-start.1 = (bf16[32,4,576]{2,1,0:T(4,128)(2,1)S(1)}, bf16[32,4,576]{2,1,0:T(4,128)(2,1)}, u32[]{:S(2)}) copy-start(bf16[32,4,576]{2,1,0:T(4,128)(2,1)} %param.16) | copy-start | bytes 442372
  297.9 9.9 %collective-permute-start.22 = (bf16[32,3584]{1,0:T(8,128)(2,1)S(1)}, bf16[32,3584]{1,0:T(8,128)(2,1)S(1)}, u32[]{:S(2)}, u32[]{:S(2)}) collective-permute-start(bf16[32,3584]{1,0:T(8,128)(2,1)S(1)} %get-tuple-element.80), channel_id=1, source_target_pairs={{0,1},{1,0},{2,3},{3,2},{4,5},{5,4},{6,7},{7,6},{8,9},{9,8},{10,11... | collective-permute-start | bytes 688136 | tf_op jit(solution)/shard_map/output_tensor1/ppermute | solution.py:511
  298.2 19.1 %collective-permute-start.23 = (bf16[32,3584]{1,0:T(8,128)(2,1)S(1)}, bf16[32,3584]{1,0:T(8,128)(2,1)S(1)}, u32[]{:S(2)}, u32[]{:S(2)}) collective-permute-start(bf16[32,3584]{1,0:T(8,128)(2,1)S(1)} %get-tuple-element.81), channel_id=1, source_target_pairs={{0,2},{1,3},{2,0},{3,1},{4,6},{5,7},{6,4},{7,5},{8,10},{9,11},{10,... | collective-permute-start | bytes 688136 | tf_op jit(solution)/shard_map/output_tensor2/ppermute | solution.py:511
  300.0 17.3 %collective-permute-start.24 = (bf16[32,3584]{1,0:T(8,128)(2,1)S(1)}, bf16[32,3584]{1,0:T(8,128)(2,1)S(1)}, u32[]{:S(2)}, u32[]{:S(2)}) collective-permute-start(bf16[32,3584]{1,0:T(8,128)(2,1)S(1)} %get-tuple-element.82), channel_id=1, source_target_pairs={{0,3},{1,2},{2,1},{3,0},{4,7},{5,6},{6,5},{7,4},{8,11},{9,10},{10,... | collective-permute-start | bytes 688136 | tf_op jit(solution)/shard_map/output_tensor3/ppermute | solution.py:511
  (29 other events, 150.6 us)
